TPU v7x, 256 devices: a whole 4x4x8 slice. The times are simulated.
256 devices in a mesh: section: 8 (over y, core), expert: 32 (over z, x).
Axes of the slice: x: 4, y: 4, z: 8, core: 2. Of those that a mesh axis runs over, the one named last changes fastest.
Arguments:
- tokens: bfloat16 [4096, 7168], P('expert', 'section'), may hold values from -6 to 6
- routes: int32 [4096, 8], P('expert'), may hold values from 0 to 63, all different within a row; in each aligned block of 128 rows (0 to 127, 128 to 255, ...) at most 24 rows name the same one
- combine: float32 [4096, 8], P('expert'), may hold values from 0.05 to 0.6
- gate_weight: bfloat16 [64, 7168, 1024], P('expert', 'section'), may hold values from -0.0625 to 0.0625
- up_weight: bfloat16 [64, 7168, 1024], P('expert', 'section'), may hold values from -0.0625 to 0.0625
- down_weight: bfloat16 [64, 1024, 7168], P('expert', None, 'section'), may hold values from -0.1875 to 0.1875
Outputs:
- mixed: bfloat16 [4096, 7168], P('expert', 'section')
Inputs may be any that keep to these rules, and one draw needn't show every extreme that they name: `routes`: among the 128 rows of one block of tokens, no expert is named more than 24 times; in every draw some expert is named exactly 24 times in some block. The 8 experts of a token differ.
All inputs are finite; a program needn't handle non-finite values.
Results may differ from a plain program's by a relative error of at most 0.029.
Values may be sent and summed in bfloat16 or wider, within the bound.
No kernel may reach another device: no remote copies, remote signals or barrier semaphores. Data moves between devices by JAX's collectives and lax.ppermute only.
A program may use at most 64 MiB of HBM per device.

v0:
```python
import functools

import jax
import jax.numpy as jnp
from jax import lax
from jax.experimental import pallas as pl
from jax.experimental.pallas import tpu as pltpu
from jax.sharding import PartitionSpec as P

BF16, F32 = jnp.bfloat16, jnp.float32
NX, CORES = 4, 2
CHUNKS = ((1, -1, 2, -2), (0, 4, 3, -3))
VMEM = pl.BlockSpec(memory_space=pltpu.VMEM)
SMEM = pl.BlockSpec(memory_space=pltpu.SMEM)
HBM = pl.BlockSpec(memory_space=pltpu.HBM)


def along_expert(value, dz, dx):
    count = lax.axis_size("expert")
    planes = count // NX
    return lax.ppermute(
        value,
        "expert",
        [(i, (i // NX + dz) % planes * NX + (i % NX + dx) % NX) for i in range(count)],
    )


def along_section(value, dy, flip):
    count = lax.axis_size("section")
    return lax.ppermute(
        value, "section", [(i, (i + CORES * dy) % count ^ flip) for i in range(count)]
    )


def call(kernel, outs, specs=None, grid=(), out_specs=None, scratch=(), limit=20, flops=0, moved=0):
    return pl.pallas_call(
        kernel,
        grid=grid,
        out_shape=outs,
        in_specs=specs,
        out_specs=out_specs or jax.tree.map(lambda _: VMEM, outs),
        scratch_shapes=scratch,
        compiler_params=pltpu.CompilerParams(vmem_limit_bytes=limit << 20),
        cost_estimate=pl.CostEstimate(flops=16 * flops, bytes_accessed=16 * moved, transcendentals=0),
    )


def pack_kernel(rows, tokens_ref, routes_ref, combine_ref, out_ref, t_ref, r_ref, c_ref, sems):
    copies = [
        pltpu.make_async_copy(src, dst, sems.at[n])
        for n, (src, dst) in enumerate(
            ((tokens_ref, t_ref), (routes_ref, r_ref), (combine_ref, c_ref))
        )
    ]
    for copy in copies:
        copy.start()
    for copy in copies:
        copy.wait()
    out_ref[pl.ds(0, rows), :] = t_ref[...]
    info = jnp.concatenate([r_ref[...].astype(F32), c_ref[...]], axis=0)
    rest = jnp.zeros((info.shape[0], out_ref.shape[1] - rows), F32)
    out_ref[pl.ds(rows, 16), :] = jnp.concatenate([info, rest], axis=1).astype(BF16)


def select_kernel(capacity, rows, at_ref, *refs):
    nz = len(refs) - 3
    blocks, (out_ref, code_ref, weight_ref) = refs[:nz], refs[nz:]
    per_plane = 2 * NX
    row = lax.broadcasted_iota(jnp.int32, (per_plane, rows), 0)
    expert = (at_ref[0] * per_plane + row).astype(F32)
    earlier = (
        lax.broadcasted_iota(jnp.int32, (rows, rows), 0)
        < lax.broadcasted_iota(jnp.int32, (rows, rows), 1)
    ).astype(F32).astype(BF16)
    codes = []
    for n, block in enumerate(blocks):
        info = block[pl.ds(rows, 16), pl.ds(0, rows)].astype(F32)
        named = jnp.zeros((per_plane, rows), F32)
        weight = jnp.zeros((per_plane, rows), F32)
        for k in range(8):
            hit = info[k : k + 1] == expert
            named = named + jnp.where(hit, 1.0, 0.0)
            weight = weight + jnp.where(hit, info[8 + k : 9 + k], 0.0)
        slot = jnp.dot(named.astype(BF16), earlier, preferred_element_type=F32)
        codes.append(jnp.where(named > 0.5, slot + float(n * capacity), -1.0))
        weight_ref[:, pl.ds(n * rows, rows)] = weight
    code = jnp.concatenate(codes, axis=1)
    code_ref[...] = code
    held = nz * capacity
    at = lax.broadcasted_iota(jnp.int32, (held, nz * rows), 0).astype(F32)
    tokens = jnp.concatenate([block[pl.ds(0, rows), :] for block in blocks], axis=0)
    for r in range(NX):
        pick = jnp.concatenate(
            [jnp.where(at == code[2 * r + e : 2 * r + e + 1], 1.0, 0.0) for e in range(2)], axis=0
        ).astype(BF16)
        out_ref[r] = jnp.dot(pick, tokens, preferred_element_type=F32).astype(BF16)


def up_kernel(held, flip, at_ref, rows_ref, gate_ref, up_ref, out_ref, x_ref, w_ref, sems):
    y = at_ref[2]
    expert = (at_ref[1] + flip) % 2
    half = gate_ref.shape[2] // 2
    pieces = [(part, c) for c in range(2) for part in range(2)]

    def fetch(n):
        part, c = pieces[n]
        return pltpu.make_async_copy(
            (gate_ref, up_ref)[part].at[expert, :, pl.ds(c * half, half)], w_ref.at[n], sems.at[n]
        )

    for n in range(4):
        fetch(n).start()
    for r in range(4):
        x_ref[pl.ds(r * held, held), :] = rows_ref[r, pl.ds(pl.multiple_of(expert * held, held), held), :]
    for n, (part, c) in enumerate(pieces):
        fetch(n).wait()
        sums = jnp.dot(x_ref[...], w_ref[n], preferred_element_type=F32).astype(BF16)
        for r in range(4):
            out_ref[(r + 4 - y) % 4, part, :, pl.ds(c * half, half)] = sums[
                r * held : (r + 1) * held
            ]


def join_kernel(keep_ref, got_ref, *outs):
    for q in range(4):
        outs[q][...] = (keep_ref[q].astype(F32) + got_ref[q].astype(F32)).astype(BF16)


def silu_kernel(a_ref, b_ref, c_ref, d_ref, out_ref):
    gate, up = (
        (a_ref[i].astype(F32) + b_ref[i].astype(F32)) + (c_ref[i].astype(F32) + d_ref[i].astype(F32))
        for i in range(2)
    )
    out_ref[...] = (jax.nn.silu(gate) * up).astype(BF16)


def down_kernel(held, at_ref, own_ref, other_ref, down_ref, out_ref, w_ref, sems):
    core, y = at_ref[1], at_ref[2]

    def fetch(n):
        return pltpu.make_async_copy(down_ref.at[(core + n) % 2], w_ref.at[n], sems.at[n])

    for n in range(2):
        fetch(n).start()
    for n, parts_ref in enumerate((own_ref, other_ref)):
        hidden = parts_ref[...].reshape(4 * held, parts_ref.shape[2])
        fetch(n).wait()
        got = jnp.dot(hidden, w_ref[n], preferred_element_type=F32).astype(BF16)
        for q in range(4):
            out_ref[(y + 4 - q) % 4, (core + n) % 2] = got[q * held : (q + 1) * held]


def mix_kernel(held, rows, back_ref, code_ref, weight_ref, *outs):
    width = code_ref.shape[1]
    at = lax.broadcasted_iota(jnp.int32, (held, width), 0).astype(F32)
    share = jnp.concatenate(
        [
            jnp.where(at == code_ref[j : j + 1, :], weight_ref[j : j + 1, :], 0.0)
            for j in range(2 * NX)
        ],
        axis=0,
    ).astype(BF16)
    total = lax.dot_general(
        share,
        back_ref[...].reshape(share.shape[0], back_ref.shape[3]),
        (((0,), (0,)), ((), ())),
        preferred_element_type=F32,
    ).astype(BF16)
    for n, out in enumerate(outs):
        out[...] = total[n * rows : (n + 1) * rows]


def shape(*dims, dtype=BF16):
    return jax.ShapeDtypeStruct(dims, dtype)


def body(tokens, routes, combine, gate_weight, up_weight, down_weight):
    groups = lax.axis_size("expert")
    per_device, width, units = gate_weight.shape
    rows, fanout = routes.shape
    capacity = 3 * rows * fanout // (2 * per_device * groups)
    place, part = lax.axis_index("expert"), lax.axis_index("section")
    at = jnp.stack([place // NX, part % CORES, part // CORES]).astype(jnp.int32)
    planes = groups // NX
    x_groups = [[z * NX + x for x in range(NX)] for z in range(planes)]
    def swap_x(value):
        return lax.all_to_all(value, "expert", 0, 0, axis_index_groups=x_groups, tiled=True)

    gate_weight, up_weight, down_weight = (
        pltpu.with_memory_space_constraint(w, pltpu.HBM)
        for w in (gate_weight, up_weight, down_weight)
    )
    block = {
        0: call(
            functools.partial(pack_kernel, rows),
            shape(rows + 16, width),
            [HBM] * 3,
            scratch=[
                pltpu.VMEM((rows, width), BF16),
                pltpu.VMEM((fanout, rows), jnp.int32),
                pltpu.VMEM((fanout, rows), F32),
                pltpu.SemaphoreType.DMA((3,)),
            ],
            moved=1 << 19,
        )(*(pltpu.with_memory_space_constraint(v, pltpu.HBM) for v in (tokens, routes.T, combine.T)))
    }
    for d in (1, -1, 2, -2):
        step = 1 if d > 0 else -1
        block[d] = along_expert(block[d - step], step, 0)
    chosen = []
    for chunk in CHUNKS:
        nz = len(chunk)
        held = nz * capacity
        if chunk == CHUNKS[1]:
            own, ahead, behind, chosen = lax.optimization_barrier(
                (block[0], block[2], block[-2], chosen)
            )
            block[3], block[-3] = along_expert(ahead, 1, 0), along_expert(behind, -1, 0)
            block[4] = along_expert(own, 4, 0)
        chosen.append(
            call(
                functools.partial(select_kernel, capacity, rows),
                [shape(4, 2 * held, width)] + [shape(2 * NX, nz * rows, dtype=F32)] * 2,
                [SMEM] + [VMEM] * nz,
                flops=16 * held * nz * rows * width,
                moved=2 << 20,
            )(at, *[block[d] for d in chunk])
        )

    def expand(came, nz):
        held = nz * capacity
        send, keep = (
            call(
                functools.partial(up_kernel, held, flip),
                shape(4, 2, held, units),
                [SMEM, VMEM, HBM, HBM],
                scratch=[
                    pltpu.VMEM((4 * held, width), BF16),
                    pltpu.VMEM((4, width, units // 2), BF16),
                    pltpu.SemaphoreType.DMA((4,)),
                ],
                flops=16 * held * width * units,
                moved=6 << 20,
            )(at, came, gate_weight, up_weight)
            for flip in (1, 0)
        )
        got = along_section(send, 0, 1)
        return call(
            join_kernel, [shape(2, held, units)] * 4, [VMEM] * 2, moved=3 << 20
        )(keep, got)

    def spread(sums):
        return [along_section(sums[q], q, 0) if q else sums[q] for q in range(4)]

    sizes = [len(chunk) for chunk in CHUNKS]
    came = [swap_x(picked) for picked, _, _ in chosen]
    terms = []
    for i, nz in enumerate(sizes):
        if i:
            came[i], sums = lax.optimization_barrier((came[i], sums))
        sums = expand(came[i], nz)
        if i:
            terms[i - 1], sums = lax.optimization_barrier((terms[i - 1], sums))
        terms.append(spread(sums))
    def activate(terms, nz):
        return call(
            silu_kernel, shape(nz * capacity, units), [VMEM] * 4, moved=1 << 20
        )(*terms)

    partials, back, hidden = [], (), activate(terms[0], sizes[0])
    for i, (chunk, (_, code, weight), nz) in enumerate(zip(CHUNKS, chosen, sizes)):
        held = nz * capacity
        pieces = [along_section(hidden, q, 0) if q else hidden for q in range(4)]
        if i + 1 < len(sizes):
            pieces, terms[i + 1], back = lax.optimization_barrier((pieces, terms[i + 1], back))
        if i:
            pieces, out = lax.optimization_barrier((pieces, out))
        parts = jnp.stack(pieces)
        others = along_section(parts, 0, 1)
        if i + 1 < len(sizes):
            hidden = activate(terms[i + 1], sizes[i + 1])
            parts, hidden = lax.optimization_barrier((parts, hidden))
        out = call(
            functools.partial(down_kernel, held),
            shape(4, 2, held, width),
            [SMEM, VMEM, VMEM, HBM],
            scratch=[pltpu.VMEM((2, units, width), BF16), pltpu.SemaphoreType.DMA((2,))],
            moved=1 << 10,
        )(at, parts, others, down_weight)
        back = swap_x(out)
        mixed = call(
            functools.partial(mix_kernel, held, rows),
            [shape(rows, width)] * nz,
            [VMEM] * 3,
            flops=16 * held * nz * rows * width,
            moved=2 << 20,
        )(back, code, weight)
        partials += [along_expert(m, -d, 0) if d else m for d, m in zip(chunk, mixed)]
    return sum(p.astype(F32) for p in partials).astype(BF16)


def solution(mesh):
    return jax.shard_map(
        body,
        mesh=mesh,
        in_specs=(
            P("expert", "section"),
            P("expert", None),
            P("expert", None),
            P("expert", "section", None),
            P("expert", "section", None),
            P("expert", None, "section"),
        ),
        out_specs=P("expert", "section"),
        check_vma=False,
    )
```

profile of v0, /device:TPU:1, one launch (start us, length us, event | category | flops | bytes accessed | tf_op | source)
XLA Modules:
  0.0 202.2 jit_solution(15856119303603859486)
XLA Ops:
  3.5 4.0 %collective-permute-start.2 = (bf16[144,896]{1,0:T(8,128)(2,1)S(1)}, bf16[144,896]{1,0:T(8,128)(2,1)S(1)}, u32[]{:S(2)}, u32[]{:S(2)}) collective-permute-start(bf16[144,896]{1,0:T(8,128)(2,1)S(1)} %shard_map.64.refs_0_), channel_id=1, source_target_pairs={{0,28},{1,29},{2,30},{3,31},{4,0},{5,1},{6,2},{7,3},{8,4},{9,5},{1... | collective-permute-start | bytes 774152 | tf_op jit(solution)/shard_map/ppermute | solution.py:21
  7.6 5.9 %collective-permute-done.refs_0_ = bf16[144,896]{1,0:T(8,128)(2,1)S(1)} collective-permute-done((bf16[144,896]{1,0:T(8,128)(2,1)S(1)}, bf16[144,896]{1,0:T(8,128)(2,1)S(1)}, u32[]{:S(2)}, u32[]{:S(2)}) %collective-permute-start) | collective-permute-done | bytes 258080 | tf_op jit(solution)/shard_map/ppermute | solution.py:21
  16.2 4.9 %collective-permute-done.1.refs_2_ = bf16[144,896]{1,0:T(8,128)(2,1)S(1)} collective-permute-done((bf16[144,896]{1,0:T(8,128)(2,1)S(1)}, bf16[144,896]{1,0:T(8,128)(2,1)S(1)}, u32[]{:S(2)}, u32[]{:S(2)}) %collective-permute-start.1) | collective-permute-done | bytes 258080 | tf_op jit(solution)/shard_map/ppermute | solution.py:21
  26.3 3.4 %collective-permute-start.8 = (bf16[144,896]{1,0:T(8,128)(2,1)S(1)}, bf16[144,896]{1,0:T(8,128)(2,1)S(1)}, u32[]{:S(2)}, u32[]{:S(2)}) collective-permute-start(bf16[144,896]{1,0:T(8,128)(2,1)S(1)} %shard_map.64.refs_0_), channel_id=1, source_target_pairs={{0,16},{1,17},{2,18},{3,19},{4,20},{5,21},{6,22},{7,23},{8,24},{9,... | collective-permute-start | bytes 774152 | tf_op jit(solution)/shard_map/ppermute | solution.py:21
  29.6 4.0 %all-to-all-start = ((bf16[4,192,896]{2,1,0:T(8,128)(2,1)}), bf16[4,192,896]{2,1,0:T(8,128)(2,1)S(1)}, u32[]{:S(2)}, u32[]{:S(2)}) async-start(bf16[4,192,896]{2,1,0:T(8,128)(2,1)} %get-tuple-element.59), calls=%async_computation | async-start | bytes 2752512 | tf_op jit(solution)/shard_map/all_to_all | solution.py:187
  33.6 7.2 %collective-permute-done.8.refs_1_ = bf16[144,896]{1,0:T(8,128)(2,1)S(1)} collective-permute-done((bf16[144,896]{1,0:T(8,128)(2,1)S(1)}, bf16[144,896]{1,0:T(8,128)(2,1)S(1)}, u32[]{:S(2)}, u32[]{:S(2)}) %collective-permute-start.8) | collective-permute-done | bytes 258080 | tf_op jit(solution)/shard_map/ppermute | solution.py:21
  40.8 4.9 %collective-permute-done.9.refs_2_ = bf16[144,896]{1,0:T(8,128)(2,1)S(1)} collective-permute-done((bf16[144,896]{1,0:T(8,128)(2,1)S(1)}, bf16[144,896]{1,0:T(8,128)(2,1)S(1)}, u32[]{:S(2)}, u32[]{:S(2)}) %collective-permute-start.9) | collective-permute-done | bytes 258080 | tf_op jit(solution)/shard_map/ppermute | solution.py:21
  45.7 2.8 %shard_map.69 = (bf16[4,192,896]{2,1,0:T(8,128)(2,1)}, f32[8,512]{1,0:T(8,128)S(1)}, f32[8,512]{1,0:T(8,128)S(1)}) custom-call(s32[3]{0:T(128)S(1)} %pad_add_fusion.at_ref, bf16[144,896]{1,0:T(8,128)(2,1)S(1)} %shard_map.64.refs_0_, bf16[144,896]{1,0:T(8,128)(2,1)S(1)} %collective-permute-done.8.refs_1_, ...), custom_call_target="tpu_custom_call" | custom-call | flops 11274289152 | bytes 33554432 | tf_op jit(solution)/shard_map/pallas_call | solution.py:221
  48.5 4.0 %all-to-all-start.1 = ((bf16[4,192,896]{2,1,0:T(8,128)(2,1)}), bf16[4,192,896]{2,1,0:T(8,128)(2,1)S(1)}, u32[]{:S(2)}, u32[]{:S(2)}) async-start(bf16[4,192,896]{2,1,0:T(8,128)(2,1)} %get-tuple-element.67), calls=%async_computation.1 | async-start | bytes 2752512 | tf_op jit(solution)/shard_map/all_to_all | solution.py:187
  52.5 4.1 %shard_map.67 = bf16[4,2,96,1024]{3,2,1,0:T(8,128)(2,1)S(1)} custom-call(s32[3]{0:T(128)S(1)} %pad_add_fusion.at_ref, bf16[4,192,896]{2,1,0:T(8,128)(2,1)S(1)} %all-to-all-done.rows_ref, bf16[2,896,1024]{2,1,0:T(8,128)(2,1)} %gate_ref.7, bf16[2,896,1024]{2,1,0:T(8,128)(2,1)} %up_ref.7), custom_call_target="tpu_custom_call" | custom-call | flops 22548578304 | bytes 100663296 | tf_op jit(solution)/shard_map/pallas_call | solution.py:233
  56.6 4.3 %collective-permute-start.4 = (bf16[4,2,96,1024]{3,2,1,0:T(8,128)(2,1)S(1)}, bf16[4,2,96,1024]{3,2,1,0:T(8,128)(2,1)S(1)}, u32[]{:S(2)}, u32[]{:S(2)}) collective-permute-start(bf16[4,2,96,1024]{3,2,1,0:T(8,128)(2,1)S(1)} %shard_map.67), channel_id=1, source_target_pairs={{0,32},{32,0},{64,96},{96,64},{128,160},{160,128},{192,224},{224,1... | collective-permute-start | bytes 4718600 | tf_op jit(solution)/shard_map/ppermute | solution.py:30
  60.9 4.1 %shard_map.66.keep_ref = bf16[4,2,96,1024]{3,2,1,0:T(8,128)(2,1)S(1)} custom-call(s32[3]{0:T(128)S(1)} %pad_add_fusion.at_ref, bf16[4,192,896]{2,1,0:T(8,128)(2,1)S(1)} %all-to-all-done.rows_ref, bf16[2,896,1024]{2,1,0:T(8,128)(2,1)} %gate_ref.7, bf16[2,896,1024]{2,1,0:T(8,128)(2,1)} %up_ref.7), custom_call_target="tpu_custom_call" | custom-call | flops 22548578304 | bytes 100663296 | tf_op jit(solution)/shard_map/pallas_call | solution.py:233
  71.2 4.1 %shard_map.71 = bf16[4,2,96,1024]{3,2,1,0:T(8,128)(2,1)S(1)} custom-call(s32[3]{0:T(128)S(1)} %pad_add_fusion.at_ref, bf16[4,192,896]{2,1,0:T(8,128)(2,1)S(1)} %all-to-all-done.1.rows_ref, bf16[2,896,1024]{2,1,0:T(8,128)(2,1)} %gate_ref.7, bf16[2,896,1024]{2,1,0:T(8,128)(2,1)} %up_ref.7), custom_call_target="tpu_custom_call" | custom-call | flops 22548578304 | bytes 100663296 | tf_op jit(solution)/shard_map/pallas_call | solution.py:233
  76.2 4.1 %shard_map.70.keep_ref = bf16[4,2,96,1024]{3,2,1,0:T(8,128)(2,1)S(1)} custom-call(s32[3]{0:T(128)S(1)} %pad_add_fusion.at_ref, bf16[4,192,896]{2,1,0:T(8,128)(2,1)S(1)} %all-to-all-done.1.rows_ref, bf16[2,896,1024]{2,1,0:T(8,128)(2,1)} %gate_ref.7, bf16[2,896,1024]{2,1,0:T(8,128)(2,1)} %up_ref.7), custom_call_target="tpu_custom_call" | custom-call | flops 22548578304 | bytes 100663296 | tf_op jit(solution)/shard_map/pallas_call | solution.py:233
  80.7 7.3 %collective-permute-done.6.c_ref = bf16[2,96,1024]{2,1,0:T(8,128)(2,1)S(1)} collective-permute-done((bf16[2,96,1024]{2,1,0:T(8,128)(2,1)}, bf16[2,96,1024]{2,1,0:T(8,128)(2,1)S(1)}, u32[]{:S(2)}, u32[]{:S(2)}) %collective-permute-start.6) | collective-permute-done | bytes 393248 | tf_op jit(solution)/shard_map/ppermute | solution.py:30
  96.4 20.8 %collective-permute-done.13 = bf16[96,1024]{1,0:T(8,128)(2,1)S(1)} collective-permute-done((bf16[96,1024]{1,0:T(8,128)(2,1)S(1)}, bf16[96,1024]{1,0:T(8,128)(2,1)S(1)}, u32[]{:S(2)}, u32[]{:S(2)}) %collective-permute-start.13) | collective-permute-done | bytes 196640 | tf_op jit(solution)/shard_map/ppermute | solution.py:30
  124.5 5.1 %shard_map.75 = bf16[4,2,96,896]{3,2,1,0:T(8,128)(2,1)} custom-call(s32[3]{0:T(128)S(1)} %pad_add_fusion.at_ref, bf16[4,96,1024]{2,1,0:T(8,128)(2,1)S(1)} %pad_maximum_fusion.own_ref, bf16[4,96,1024]{2,1,0:T(8,128)(2,1)S(1)} %collective-permute-done.18.other_ref, bf16[2,1024,896]{2,1,0:T(8,128)(2,1)} %down_ref.3), custom_call_target="tpu_custom_call" | custom-call | bytes 16384 | tf_op jit(solution)/shard_map/pallas_call | solution.py:283
  129.6 4.5 %all-to-all-start.2 = ((bf16[4,2,96,896]{3,2,1,0:T(8,128)(2,1)}), bf16[4,2,96,896]{3,2,1,0:T(8,128)(2,1)S(1)}, u32[]{:S(2)}, u32[]{:S(2)}) async-start(bf16[4,2,96,896]{3,2,1,0:T(8,128)(2,1)} %shard_map.75), calls=%async_computation.2 | async-start | bytes 2752512 | tf_op jit(solution)/shard_map/all_to_all | solution.py:187
  137.4 5.2 %shard_map.77 = bf16[4,2,96,896]{3,2,1,0:T(8,128)(2,1)} custom-call(s32[3]{0:T(128)S(1)} %pad_add_fusion.at_ref, bf16[4,96,1024]{2,1,0:T(8,128)(2,1)S(1)} %pad_maximum_fusion.1.own_ref, bf16[4,96,1024]{2,1,0:T(8,128)(2,1)S(1)} %collective-permute-done.26.other_ref, bf16[2,1024,896]{2,1,0:T(8,128)(2,1)} %down_ref.3), custom_call_target="tpu_custom_call" | custom-call | bytes 16384 | tf_op jit(solution)/shard_map/pallas_call | solution.py:283
  142.6 9.0 %all-to-all-done.2.back_ref = bf16[4,2,96,896]{3,2,1,0:T(8,128)(2,1)S(1)} async-done(((bf16[4,2,96,896]{3,2,1,0:T(8,128)(2,1)}), bf16[4,2,96,896]{3,2,1,0:T(8,128)(2,1)S(1)}, u32[]{:S(2)}, u32[]{:S(2)}) %all-to-all-start.2) | async-done | bytes 1376288 | tf_op jit(solution)/shard_map/all_to_all | solution.py:187
  151.6 3.5 %all-to-all-start.3 = ((bf16[4,2,96,896]{3,2,1,0:T(8,128)(2,1)}), bf16[4,2,96,896]{3,2,1,0:T(8,128)(2,1)S(1)}, u32[]{:S(2)}, u32[]{:S(2)}) async-start(bf16[4,2,96,896]{3,2,1,0:T(8,128)(2,1)} %shard_map.77), calls=%async_computation.3 | async-start | bytes 2752512 | tf_op jit(solution)/shard_map/all_to_all | solution.py:187
  161.8 9.9 %all-to-all-done.3.back_ref = bf16[4,2,96,896]{3,2,1,0:T(8,128)(2,1)S(1)} async-done(((bf16[4,2,96,896]{3,2,1,0:T(8,128)(2,1)}), bf16[4,2,96,896]{3,2,1,0:T(8,128)(2,1)S(1)}, u32[]{:S(2)}, u32[]{:S(2)}) %all-to-all-start.3) | async-done | bytes 1376288 | tf_op jit(solution)/shard_map/all_to_all | solution.py:187
  178.6 10.2 %collective-permute-done.27 = bf16[128,896]{1,0:T(8,128)(2,1)S(1)} collective-permute-done((bf16[128,896]{1,0:T(8,128)(2,1)S(1)}, bf16[128,896]{1,0:T(8,128)(2,1)S(1)}, u32[]{:S(2)}, u32[]{:S(2)}) %collective-permute-start.27) | collective-permute-done | bytes 229408 | tf_op jit(solution)/shard_map/ppermute | solution.py:21
  188.8 11.4 %collective-permute-done.28 = bf16[128,896]{1,0:T(8,128)(2,1)S(1)} collective-permute-done((bf16[128,896]{1,0:T(8,128)(2,1)S(1)}, bf16[128,896]{1,0:T(8,128)(2,1)S(1)}, u32[]{:S(2)}, u32[]{:S(2)}) %collective-permute-start.28) | collective-permute-done | bytes 229408 | tf_op jit(solution)/shard_map/ppermute | solution.py:21
  (63 shorter events, 53.4 us)
Async XLA Ops:
  1.0 12.4 %collective-permute-start = (bf16[144,896]{1,0:T(8,128)(2,1)S(1)}, bf16[144,896]{1,0:T(8,128)(2,1)S(1)}, u32[]{:S(2)}, u32[]{:S(2)}) collective-permute-start(bf16[144,896]{1,0:T(8,128)(2,1)S(1)} %shard_map.64.refs_0_), channel_id=1, source_target_pairs={{0,4},{1,5},{2,6},{3,7},{4,8},{5,9},{6,10},{7,11},{8,12},{9,13},{1... | collective-permute-start | bytes 774152 | tf_op jit(solution)/shard_map/ppermute | solution.py:21
  26.3 14.5 %collective-permute-start.8 = (bf16[144,896]{1,0:T(8,128)(2,1)S(1)}, bf16[144,896]{1,0:T(8,128)(2,1)S(1)}, u32[]{:S(2)}, u32[]{:S(2)}) collective-permute-start(bf16[144,896]{1,0:T(8,128)(2,1)S(1)} %shard_map.64.refs_0_), channel_id=1, source_target_pairs={{0,16},{1,17},{2,18},{3,19},{4,20},{5,21},{6,22},{7,23},{8,24},{9,... | collective-permute-start | bytes 774152 | tf_op jit(solution)/shard_map/ppermute | solution.py:21
  29.6 16.1 %collective-permute-start.9 = (bf16[144,896]{1,0:T(8,128)(2,1)S(1)}, bf16[144,896]{1,0:T(8,128)(2,1)S(1)}, u32[]{:S(2)}, u32[]{:S(2)}) collective-permute-start(bf16[144,896]{1,0:T(8,128)(2,1)S(1)} %collective-permute-done.1.refs_2_), channel_id=1, source_target_pairs={{0,4},{1,5},{2,6},{3,7},{4,8},{5,9},{6,10},{7,11},{8,12},{9,13},{1... | collective-permute-start | bytes 774152 | tf_op jit(solution)/shard_map/ppermute | solution.py:21
  29.6 18.9 %all-to-all-start = ((bf16[4,192,896]{2,1,0:T(8,128)(2,1)}), bf16[4,192,896]{2,1,0:T(8,128)(2,1)S(1)}, u32[]{:S(2)}, u32[]{:S(2)}) async-start(bf16[4,192,896]{2,1,0:T(8,128)(2,1)} %get-tuple-element.59), calls=%async_computation | async-start | bytes 2752512 | tf_op jit(solution)/shard_map/all_to_all | solution.py:187
  48.5 22.6 %all-to-all-start.1 = ((bf16[4,192,896]{2,1,0:T(8,128)(2,1)}), bf16[4,192,896]{2,1,0:T(8,128)(2,1)S(1)}, u32[]{:S(2)}, u32[]{:S(2)}) async-start(bf16[4,192,896]{2,1,0:T(8,128)(2,1)} %get-tuple-element.67), calls=%async_computation.1 | async-start | bytes 2752512 | tf_op jit(solution)/shard_map/all_to_all | solution.py:187
  66.2 14.5 %collective-permute-start.5 = (bf16[2,96,1024]{2,1,0:T(8,128)(2,1)}, bf16[2,96,1024]{2,1,0:T(8,128)(2,1)S(1)}, u32[]{:S(2)}, u32[]{:S(2)}) collective-permute-start(bf16[2,96,1024]{2,1,0:T(8,128)(2,1)} %get-tuple-element.61), channel_id=1, source_target_pairs={{0,64},{32,96},{64,128},{96,160},{128,192},{160,224},{192,0},{224,... | collective-permute-start | bytes 1179656 | tf_op jit(solution)/shard_map/ppermute | solution.py:30
  67.5 20.5 %collective-permute-start.6 = (bf16[2,96,1024]{2,1,0:T(8,128)(2,1)}, bf16[2,96,1024]{2,1,0:T(8,128)(2,1)S(1)}, u32[]{:S(2)}, u32[]{:S(2)}) collective-permute-start(bf16[2,96,1024]{2,1,0:T(8,128)(2,1)} %get-tuple-element.62), channel_id=1, source_target_pairs={{0,128},{32,160},{64,192},{96,224},{128,0},{160,32},{192,64},{224,... | collective-permute-start | bytes 1179656 | tf_op jit(solution)/shard_map/ppermute | solution.py:30
  70.1 17.9 %collective-permute-start.7 = (bf16[2,96,1024]{2,1,0:T(8,128)(2,1)S(1)}, bf16[2,96,1024]{2,1,0:T(8,128)(2,1)S(1)}, u32[]{:S(2)}, u32[]{:S(2)}) collective-permute-start(bf16[2,96,1024]{2,1,0:T(8,128)(2,1)S(1)} %get-tuple-element.63), channel_id=1, source_target_pairs={{0,192},{32,224},{64,0},{96,32},{128,64},{160,96},{192,128},{224,1... | collective-permute-start | bytes 1179656 | tf_op jit(solution)/shard_map/ppermute | solution.py:30
  88.4 28.8 %collective-permute-start.15 = (bf16[2,96,1024]{2,1,0:T(8,128)(2,1)S(1)}, bf16[2,96,1024]{2,1,0:T(8,128)(2,1)S(1)}, u32[]{:S(2)}, u32[]{:S(2)}) collective-permute-start(bf16[2,96,1024]{2,1,0:T(8,128)(2,1)S(1)} %get-tuple-element.78), channel_id=1, source_target_pairs={{0,64},{32,96},{64,128},{96,160},{128,192},{160,224},{192,0},{224,... | collective-permute-start | bytes 1179656 | tf_op jit(solution)/shard_map/ppermute | solution.py:30
  90.0 27.2 %collective-permute-start.16 = (bf16[2,96,1024]{2,1,0:T(8,128)(2,1)S(1)}, bf16[2,96,1024]{2,1,0:T(8,128)(2,1)S(1)}, u32[]{:S(2)}, u32[]{:S(2)}) collective-permute-start(bf16[2,96,1024]{2,1,0:T(8,128)(2,1)S(1)} %get-tuple-element.79), channel_id=1, source_target_pairs={{0,128},{32,160},{64,192},{96,224},{128,0},{160,32},{192,64},{224,... | collective-permute-start | bytes 1179656 | tf_op jit(solution)/shard_map/ppermute | solution.py:30
  92.2 25.0 %collective-permute-start.17 = (bf16[2,96,1024]{2,1,0:T(8,128)(2,1)S(1)}, bf16[2,96,1024]{2,1,0:T(8,128)(2,1)S(1)}, u32[]{:S(2)}, u32[]{:S(2)}) collective-permute-start(bf16[2,96,1024]{2,1,0:T(8,128)(2,1)S(1)} %get-tuple-element.80), channel_id=1, source_target_pairs={{0,192},{32,224},{64,0},{96,32},{128,64},{160,96},{192,128},{224,1... | collective-permute-start | bytes 1179656 | tf_op jit(solution)/shard_map/ppermute | solution.py:30
  93.7 23.5 %collective-permute-start.13 = (bf16[96,1024]{1,0:T(8,128)(2,1)S(1)}, bf16[96,1024]{1,0:T(8,128)(2,1)S(1)}, u32[]{:S(2)}, u32[]{:S(2)}) collective-permute-start(bf16[96,1024]{1,0:T(8,128)(2,1)S(1)} %shard_map.73), channel_id=1, source_target_pairs={{0,128},{32,160},{64,192},{96,224},{128,0},{160,32},{192,64},{224,... | collective-permute-start | bytes 589832 | tf_op jit(solution)/shard_map/ppermute | solution.py:30
  95.2 22.0 %collective-permute-start.14 = (bf16[96,1024]{1,0:T(8,128)(2,1)S(1)}, bf16[96,1024]{1,0:T(8,128)(2,1)S(1)}, u32[]{:S(2)}, u32[]{:S(2)}) collective-permute-start(bf16[96,1024]{1,0:T(8,128)(2,1)S(1)} %shard_map.73), channel_id=1, source_target_pairs={{0,192},{32,224},{64,0},{96,32},{128,64},{160,96},{192,128},{224,1... | collective-permute-start | bytes 589832 | tf_op jit(solution)/shard_map/ppermute | solution.py:30
  119.1 15.0 %collective-permute-start.23 = (bf16[96,1024]{1,0:T(8,128)(2,1)S(1)}, bf16[96,1024]{1,0:T(8,128)(2,1)S(1)}, u32[]{:S(2)}, u32[]{:S(2)}) collective-permute-start(bf16[96,1024]{1,0:T(8,128)(2,1)S(1)} %shard_map.74), channel_id=1, source_target_pairs={{0,64},{32,96},{64,128},{96,160},{128,192},{160,224},{192,0},{224,... | collective-permute-start | bytes 589832 | tf_op jit(solution)/shard_map/ppermute | solution.py:30
  120.6 13.5 %collective-permute-start.24 = (bf16[96,1024]{1,0:T(8,128)(2,1)S(1)}, bf16[96,1024]{1,0:T(8,128)(2,1)S(1)}, u32[]{:S(2)}, u32[]{:S(2)}) collective-permute-start(bf16[96,1024]{1,0:T(8,128)(2,1)S(1)} %shard_map.74), channel_id=1, source_target_pairs={{0,128},{32,160},{64,192},{96,224},{128,0},{160,32},{192,64},{224,... | collective-permute-start | bytes 589832 | tf_op jit(solution)/shard_map/ppermute | solution.py:30
  129.6 22.0 %all-to-all-start.2 = ((bf16[4,2,96,896]{3,2,1,0:T(8,128)(2,1)}), bf16[4,2,96,896]{3,2,1,0:T(8,128)(2,1)S(1)}, u32[]{:S(2)}, u32[]{:S(2)}) async-start(bf16[4,2,96,896]{3,2,1,0:T(8,128)(2,1)} %shard_map.75), calls=%async_computation.2 | async-start | bytes 2752512 | tf_op jit(solution)/shard_map/all_to_all | solution.py:187
  151.6 20.1 %all-to-all-start.3 = ((bf16[4,2,96,896]{3,2,1,0:T(8,128)(2,1)}), bf16[4,2,96,896]{3,2,1,0:T(8,128)(2,1)S(1)}, u32[]{:S(2)}, u32[]{:S(2)}) async-start(bf16[4,2,96,896]{3,2,1,0:T(8,128)(2,1)} %shard_map.77), calls=%async_computation.3 | async-start | bytes 2752512 | tf_op jit(solution)/shard_map/all_to_all | solution.py:187
  156.8 18.0 %collective-permute-start.19 = (bf16[128,896]{1,0:T(8,128)(2,1)}, bf16[128,896]{1,0:T(8,128)(2,1)S(1)}, u32[]{:S(2)}, u32[]{:S(2)}) collective-permute-start(bf16[128,896]{1,0:T(8,128)(2,1)} %get-tuple-element.92), channel_id=1, source_target_pairs={{0,28},{1,29},{2,30},{3,31},{4,0},{5,1},{6,2},{7,3},{8,4},{9,5},{1... | collective-permute-start | bytes 688136 | tf_op jit(solution)/shard_map/ppermute | solution.py:21
  159.4 16.6 %collective-permute-start.20 = (bf16[128,896]{1,0:T(8,128)(2,1)S(1)}, bf16[128,896]{1,0:T(8,128)(2,1)S(1)}, u32[]{:S(2)}, u32[]{:S(2)}) collective-permute-start(bf16[128,896]{1,0:T(8,128)(2,1)S(1)} %get-tuple-element.93), channel_id=1, source_target_pairs={{0,4},{1,5},{2,6},{3,7},{4,8},{5,9},{6,10},{7,11},{8,12},{9,13},{1... | collective-permute-start | bytes 688136 | tf_op jit(solution)/shard_map/ppermute | solution.py:21
  159.4 19.1 %collective-permute-start.21 = (bf16[128,896]{1,0:T(8,128)(2,1)S(1)}, bf16[128,896]{1,0:T(8,128)(2,1)S(1)}, u32[]{:S(2)}, u32[]{:S(2)}) collective-permute-start(bf16[128,896]{1,0:T(8,128)(2,1)S(1)} %get-tuple-element.94), channel_id=1, source_target_pairs={{0,24},{1,25},{2,26},{3,27},{4,28},{5,29},{6,30},{7,31},{8,0},{9,1... | collective-permute-start | bytes 688136 | tf_op jit(solution)/shard_map/ppermute | solution.py:21
  160.6 17.9 %collective-permute-start.22 = (bf16[128,896]{1,0:T(8,128)(2,1)S(1)}, bf16[128,896]{1,0:T(8,128)(2,1)S(1)}, u32[]{:S(2)}, u32[]{:S(2)}) collective-permute-start(bf16[128,896]{1,0:T(8,128)(2,1)S(1)} %get-tuple-element.95), channel_id=1, source_target_pairs={{0,8},{1,9},{2,10},{3,11},{4,12},{5,13},{6,14},{7,15},{8,16},{9,17... | collective-permute-start | bytes 688136 | tf_op jit(solution)/shard_map/ppermute | solution.py:21
  172.7 16.1 %collective-permute-start.27 = (bf16[128,896]{1,0:T(8,128)(2,1)S(1)}, bf16[128,896]{1,0:T(8,128)(2,1)S(1)}, u32[]{:S(2)}, u32[]{:S(2)}) collective-permute-start(bf16[128,896]{1,0:T(8,128)(2,1)S(1)} %get-tuple-element.104), channel_id=1, source_target_pairs={{0,16},{1,17},{2,18},{3,19},{4,20},{5,21},{6,22},{7,23},{8,24},{9,... | collective-permute-start | bytes 688136 | tf_op jit(solution)/shard_map/ppermute | solution.py:21
  174.8 25.4 %collective-permute-start.28 = (bf16[128,896]{1,0:T(8,128)(2,1)S(1)}, bf16[128,896]{1,0:T(8,128)(2,1)S(1)}, u32[]{:S(2)}, u32[]{:S(2)}) collective-permute-start(bf16[128,896]{1,0:T(8,128)(2,1)S(1)} %get-tuple-element.105), channel_id=1, source_target_pairs={{0,20},{1,21},{2,22},{3,23},{4,24},{5,25},{6,26},{7,27},{8,28},{9,... | collective-permute-start | bytes 688136 | tf_op jit(solution)/shard_map/ppermute | solution.py:21
  176.1 25.2 %collective-permute-start.29 = (bf16[128,896]{1,0:T(8,128)(2,1)S(1)}, bf16[128,896]{1,0:T(8,128)(2,1)S(1)}, u32[]{:S(2)}, u32[]{:S(2)}) collective-permute-start(bf16[128,896]{1,0:T(8,128)(2,1)S(1)} %get-tuple-element.106), channel_id=1, source_target_pairs={{0,12},{1,13},{2,14},{3,15},{4,16},{5,17},{6,18},{7,19},{8,20},{9,... | collective-permute-start | bytes 688136 | tf_op jit(solution)/shard_map/ppermute | solution.py:21
  (10 other events, 77.2 us)
where the time goes:
time: 203 us; the launch traced here: 202 us
  waiting for transfers between devices  96.1 us (47%)
  starting transfers between devices  67 us (33%)
  Pallas kernels  37.7 us (19%)
    ppermute x14, waiting for transfers between devices, along_expert(): lax.ppermute(value, 'expert', [(i, (i // NX + dz) % planes * NX + (i % NX...  45.6 us
    ppermute x16, waiting for transfers between devices, along_section(): lax.ppermute(value, 'section', [(i, (i + CORES * dy) % count ^ flip) for...  31.5 us
    ppermute x14, starting transfers between devices, along_expert(): lax.ppermute(value, 'expert', [(i, (i // NX + dz) % planes * NX + (i % NX...  25.9 us
    ppermute x16, starting transfers between devices, along_section(): lax.ppermute(value, 'section', [(i, (i + CORES * dy) % count ^ flip) for...  25.1 us
    all_to_all x4, waiting for transfers between devices, swap_x(): lax.all_to_all(value, 'expert', 0, 0, axis_index_groups=x_groups, tiled=T...  18.9 us
    pallas_call x4, Pallas kernels, expand(): call(functools.partial(up_kernel, held, flip), shape(4, 2, held, units),...  16.2 us
    all_to_all x4, starting transfers between devices, swap_x(): lax.all_to_all(value, 'expert', 0, 0, axis_index_groups=x_groups, tiled=T...  16.1 us
    pallas_call x2, Pallas kernels, body(): call(functools.partial(down_kernel, held), shape(4, 2, held, width), [SME...  10.4 us
  transfers between devices with their start and end apart: 34, of which 13 were waited for; matrix products, arithmetic and copies ran while one was open for 0% of the time, Pallas kernels for 17%

commit v1 on v0

--- a/solution.py
+++ b/solution.py
@@ -126,16 +126,30 @@
         outs[q][...] = (keep_ref[q].astype(F32) + got_ref[q].astype(F32)).astype(BF16)
 
 
-def silu_kernel(a_ref, b_ref, c_ref, d_ref, out_ref):
+def activate(terms):
     gate, up = (
-        (a_ref[i].astype(F32) + b_ref[i].astype(F32)) + (c_ref[i].astype(F32) + d_ref[i].astype(F32))
+        (terms[0][i].astype(F32) + terms[1][i].astype(F32))
+        + (terms[2][i].astype(F32) + terms[3][i].astype(F32))
         for i in range(2)
     )
-    out_ref[...] = (jax.nn.silu(gate) * up).astype(BF16)
-
-
-def down_kernel(held, at_ref, own_ref, other_ref, down_ref, out_ref, w_ref, sems):
-    core, y = at_ref[1], at_ref[2]
+    return (jax.nn.silu(gate) * up).astype(BF16)
+
+
+def silu_kernel(*refs):
+    refs[4][...] = activate(refs[:4])
+
+
+def turn_kernel(*refs):
+    terms, (keep_ref, got_ref), outs = refs[:4], refs[4:6], refs[6:]
+    hidden = activate(terms)
+    for q in range(4):
+        outs[q][pl.ds(0, 2)] = (keep_ref[q].astype(F32) + got_ref[q].astype(F32)).astype(BF16)
+        outs[q][2] = hidden
+
+
+def down_kernel(held, at_ref, own_ref, other_ref, down_ref, *refs):
+    outs, (h_ref, w_ref, sems) = refs[:4], refs[4:]
+    core, y, x = at_ref[1], at_ref[2], at_ref[3]
 
     def fetch(n):
         return pltpu.make_async_copy(down_ref.at[(core + n) % 2], w_ref.at[n], sems.at[n])
@@ -143,26 +157,27 @@
     for n in range(2):
         fetch(n).start()
     for n, parts_ref in enumerate((own_ref, other_ref)):
-        hidden = parts_ref[...].reshape(4 * held, parts_ref.shape[2])
+        for d in range(4):
+            h_ref[pl.ds(d * held, held), :] = parts_ref[(y + 8 - x - d) % 4]
         fetch(n).wait()
-        got = jnp.dot(hidden, w_ref[n], preferred_element_type=F32).astype(BF16)
-        for q in range(4):
-            out_ref[(y + 4 - q) % 4, (core + n) % 2] = got[q * held : (q + 1) * held]
-
-
-def mix_kernel(held, rows, back_ref, code_ref, weight_ref, *outs):
+        got = jnp.dot(h_ref[...], w_ref[n], preferred_element_type=F32).astype(BF16)
+        for d in range(4):
+            outs[d][(core + n) % 2] = got[d * held : (d + 1) * held]
+
+
+def mix_kernel(held, rows, at_ref, *refs):
+    backs, (code_ref, weight_ref), outs = refs[:4], refs[4:6], refs[6:]
     width = code_ref.shape[1]
     at = lax.broadcasted_iota(jnp.int32, (held, width), 0).astype(F32)
-    share = jnp.concatenate(
-        [
-            jnp.where(at == code_ref[j : j + 1, :], weight_ref[j : j + 1, :], 0.0)
-            for j in range(2 * NX)
-        ],
-        axis=0,
-    ).astype(BF16)
+    share = []
+    for d in range(4):
+        for e in range(2):
+            j = pl.ds((at_ref[3] + 4 - d) % 4 * 2 + e, 1)
+            share.append(jnp.where(at == code_ref[j, :], weight_ref[j, :], 0.0))
+    back = jnp.concatenate([backs[d][e] for d in range(4) for e in range(2)], axis=0)
     total = lax.dot_general(
-        share,
-        back_ref[...].reshape(share.shape[0], back_ref.shape[3]),
+        jnp.concatenate(share, axis=0).astype(BF16),
+        back,
         (((0,), (0,)), ((), ())),
         preferred_element_type=F32,
     ).astype(BF16)
@@ -180,7 +195,7 @@
     rows, fanout = routes.shape
     capacity = 3 * rows * fanout // (2 * per_device * groups)
     place, part = lax.axis_index("expert"), lax.axis_index("section")
-    at = jnp.stack([place // NX, part % CORES, part // CORES]).astype(jnp.int32)
+    at = jnp.stack([place // NX, part % CORES, part // CORES, place % NX]).astype(jnp.int32)
     planes = groups // NX
     x_groups = [[z * NX + x for x in range(NX)] for z in range(planes)]
     def swap_x(value):
@@ -227,8 +242,7 @@
             )(at, *[block[d] for d in chunk])
         )
 
-    def expand(came, nz):
-        held = nz * capacity
+    def expand(came):
         send, keep = (
             call(
                 functools.partial(up_kernel, held, flip),
@@ -244,58 +258,58 @@
             )(at, came, gate_weight, up_weight)
             for flip in (1, 0)
         )
-        got = along_section(send, 0, 1)
-        return call(
-            join_kernel, [shape(2, held, units)] * 4, [VMEM] * 2, moved=3 << 20
-        )(keep, got)
-
-    def spread(sums):
-        return [along_section(sums[q], q, 0) if q else sums[q] for q in range(4)]
-
-    sizes = [len(chunk) for chunk in CHUNKS]
-    came = [swap_x(picked) for picked, _, _ in chosen]
-    terms = []
-    for i, nz in enumerate(sizes):
-        if i:
-            came[i], sums = lax.optimization_barrier((came[i], sums))
-        sums = expand(came[i], nz)
-        if i:
-            terms[i - 1], sums = lax.optimization_barrier((terms[i - 1], sums))
-        terms.append(spread(sums))
-    def activate(terms, nz):
-        return call(
-            silu_kernel, shape(nz * capacity, units), [VMEM] * 4, moved=1 << 20
-        )(*terms)
-
-    partials, back, hidden = [], (), activate(terms[0], sizes[0])
-    for i, (chunk, (_, code, weight), nz) in enumerate(zip(CHUNKS, chosen, sizes)):
-        held = nz * capacity
-        pieces = [along_section(hidden, q, 0) if q else hidden for q in range(4)]
-        if i + 1 < len(sizes):
-            pieces, terms[i + 1], back = lax.optimization_barrier((pieces, terms[i + 1], back))
-        if i:
-            pieces, out = lax.optimization_barrier((pieces, out))
-        parts = jnp.stack(pieces)
-        others = along_section(parts, 0, 1)
-        if i + 1 < len(sizes):
-            hidden = activate(terms[i + 1], sizes[i + 1])
-            parts, hidden = lax.optimization_barrier((parts, hidden))
+        return keep, along_section(send, 0, 1)
+
+    def spread(values):
+        return [along_section(v, q, 0) if q else v for q, v in enumerate(values)]
+
+    def contract(parts, others):
         out = call(
             functools.partial(down_kernel, held),
-            shape(4, 2, held, width),
+            [shape(2, held, width)] * 4,
             [SMEM, VMEM, VMEM, HBM],
-            scratch=[pltpu.VMEM((2, units, width), BF16), pltpu.SemaphoreType.DMA((2,))],
+            scratch=[
+                pltpu.VMEM((4 * held, units), BF16),
+                pltpu.VMEM((2, units, width), BF16),
+                pltpu.SemaphoreType.DMA((2,)),
+            ],
             moved=1 << 10,
         )(at, parts, others, down_weight)
-        back = swap_x(out)
+        return out, [along_expert(v, 0, d) if d else v for d, v in enumerate(out)]
+
+    def mix(chunk, back, code, weight):
         mixed = call(
             functools.partial(mix_kernel, held, rows),
-            [shape(rows, width)] * nz,
-            [VMEM] * 3,
-            flops=16 * held * nz * rows * width,
+            [shape(rows, width)] * len(chunk),
+            [SMEM] + [VMEM] * 6,
+            flops=16 * held * len(chunk) * rows * width,
             moved=2 << 20,
-        )(back, code, weight)
-        partials += [along_expert(m, -d, 0) if d else m for d, m in zip(chunk, mixed)]
+        )(at, *back, code, weight)
+        return [along_expert(m, -d, 0) if d else m for d, m in zip(chunk, mixed)]
+
+    near, far = CHUNKS
+    held = len(near) * capacity
+    (first, *first_codes), (second, *second_codes) = chosen
+    came = swap_x(first)
+    came_second = swap_x(second)
+    sums = call(join_kernel, [shape(2, held, units)] * 4, [VMEM] * 2, moved=3 << 20)(*expand(came))
+    came_second, _ = lax.optimization_barrier((came_second, sums))
+    keep, got = expand(came_second)
+    terms = spread(sums)
+    mail = spread(
+        call(turn_kernel, [shape(3, held, units)] * 4, [VMEM] * 6, moved=3 << 20)(*terms, keep, got)
+    )
+    parts = jnp.stack([m[2] for m in mail])
+    others = along_section(parts, 0, 1)
+    hidden = call(silu_kernel, shape(held, units), [VMEM] * 4, moved=1 << 20)(*mail)
+    parts, hidden = lax.optimization_barrier((parts, hidden))
+    pieces = spread([hidden] * 4)
+    out, back = contract(parts, others)
+    pieces, out = lax.optimization_barrier((pieces, out))
+    parts = jnp.stack(pieces)
+    others = along_section(parts, 0, 1)
+    _, back_second = contract(parts, others)
+    partials = mix(near, back, *first_codes) + mix(far, back_second, *second_codes)
     return sum(p.astype(F32) for p in partials).astype(BF16)
 
 

time: 203 us -> 209 us (1.030)
  waiting for transfers between devices: 96.1 us -> 113 us
  starting transfers between devices: 67 us -> 58.5 us
    ppermute x14 -> x20, waiting for transfers between devices: 45.6 us -> 69.7 us  [along_expert(): lax.ppermute(value, 'expert', [(i, (i // NX + dz) % planes * NX + (i % NX...]
    all_to_all x4 -> x2, waiting for transfers between devices: 18.9 us -> 2.6 us  [swap_x(): lax.all_to_all(value, 'expert', 0, 0, axis_index_groups=x_groups, tiled=T...]
    ppermute x16 -> x13, waiting for transfers between devices: 31.5 us -> 40.2 us  [along_section(): lax.ppermute(value, 'section', [(i, (i + CORES * dy) % count ^ flip) for...]
    all_to_all x4 -> x2, starting transfers between devices: 16.1 us -> 7.56 us  [swap_x(): lax.all_to_all(value, 'expert', 0, 0, axis_index_groups=x_groups, tiled=T...]
    ppermute x16 -> x13, starting transfers between devices: 25.1 us -> 20.2 us  [along_section(): lax.ppermute(value, 'section', [(i, (i + CORES * dy) % count ^ flip) for...]
    ppermute x14 -> x20, starting transfers between devices: 25.9 us -> 30.7 us  [along_expert(): lax.ppermute(value, 'expert', [(i, (i // NX + dz) % planes * NX + (i % NX...]
    pallas_call x8 -> x7, Pallas kernels: 15 us -> 13.3 us  [the longest x2 8.15 us: contract(): call(functools.partial(down_kernel, held), [shape(2, held, width)] * 4, [...]
  transfers between devices with their start and end apart: 34 -> 35, of which waited for: 13 -> 19; matrix products, arithmetic and copies ran while one was open for 0% -> 0% of each run, Pallas kernels for 17% -> 15%
where the time goes in v1:
time: 209 us
  waiting for transfers between devices  113 us (54%)
  starting transfers between devices  58.5 us (28%)
  Pallas kernels  36 us (17%)
    ppermute x20, waiting for transfers between devices, along_expert(): lax.ppermute(value, 'expert', [(i, (i // NX + dz) % planes * NX + (i % NX...  69.7 us
    ppermute x13, waiting for transfers between devices, along_section(): lax.ppermute(value, 'section', [(i, (i + CORES * dy) % count ^ flip) for...  40.2 us
    ppermute x20, starting transfers between devices, along_expert(): lax.ppermute(value, 'expert', [(i, (i // NX + dz) % planes * NX + (i % NX...  30.7 us
    ppermute x13, starting transfers between devices, along_section(): lax.ppermute(value, 'section', [(i, (i + CORES * dy) % count ^ flip) for...  20.2 us
    pallas_call x4, Pallas kernels, expand(): call(functools.partial(up_kernel, held, flip), shape(4, 2, held, units),...  16.2 us
    pallas_call x2, Pallas kernels, contract(): call(functools.partial(down_kernel, held), [shape(2, held, width)] * 4, [...  8.15 us
    all_to_all x2, starting transfers between devices, swap_x(): lax.all_to_all(value, 'expert', 0, 0, axis_index_groups=x_groups, tiled=T...  7.56 us
    pallas_call x2, Pallas kernels, body(): call(functools.partial(select_kernel, capacity, rows), [shape(4, 2 * held...  5.52 us
  transfers between devices with their start and end apart: 35, of which 19 were waited for; matrix products, arithmetic and copies ran while one was open for 0% of the time, Pallas kernels for 15%

profile of v1, /device:TPU:1, one launch (start us, length us, event | category | flops | bytes accessed | tf_op | source)
XLA Modules:
  0.0 208.5 jit_solution(16290674725441952897)
XLA Ops:
  1.0 6.5 %collective-permute-start.2 = (bf16[144,896]{1,0:T(8,128)(2,1)S(1)}, bf16[144,896]{1,0:T(8,128)(2,1)S(1)}, u32[]{:S(2)}, u32[]{:S(2)}) collective-permute-start(bf16[144,896]{1,0:T(8,128)(2,1)S(1)} %shard_map.64.refs_0_), channel_id=1, source_target_pairs={{0,28},{1,29},{2,30},{3,31},{4,0},{5,1},{6,2},{7,3},{8,4},{9,5},{1... | collective-permute-start | bytes 774152 | tf_op jit(solution)/shard_map/ppermute | solution.py:21
  7.5 4.9 %collective-permute-done.2.refs_1_ = bf16[144,896]{1,0:T(8,128)(2,1)S(1)} collective-permute-done((bf16[144,896]{1,0:T(8,128)(2,1)S(1)}, bf16[144,896]{1,0:T(8,128)(2,1)S(1)}, u32[]{:S(2)}, u32[]{:S(2)}) %collective-permute-start.2) | collective-permute-done | bytes 258080 | tf_op jit(solution)/shard_map/ppermute | solution.py:21
  15.9 3.9 %collective-permute-done.3.refs_3_ = bf16[144,896]{1,0:T(8,128)(2,1)S(1)} collective-permute-done((bf16[144,896]{1,0:T(8,128)(2,1)S(1)}, bf16[144,896]{1,0:T(8,128)(2,1)S(1)}, u32[]{:S(2)}, u32[]{:S(2)}) %collective-permute-start.3) | collective-permute-done | bytes 258080 | tf_op jit(solution)/shard_map/ppermute | solution.py:21
  30.0 4.0 %all-to-all-start = ((bf16[4,192,896]{2,1,0:T(8,128)(2,1)}), bf16[4,192,896]{2,1,0:T(8,128)(2,1)S(1)}, u32[]{:S(2)}, u32[]{:S(2)}) async-start(bf16[4,192,896]{2,1,0:T(8,128)(2,1)} %get-tuple-element.51), calls=%async_computation | async-start | bytes 2752512 | tf_op jit(solution)/shard_map/all_to_all | solution.py:202
  34.0 6.1 %collective-permute-done.8.refs_1_ = bf16[144,896]{1,0:T(8,128)(2,1)S(1)} collective-permute-done((bf16[144,896]{1,0:T(8,128)(2,1)S(1)}, bf16[144,896]{1,0:T(8,128)(2,1)S(1)}, u32[]{:S(2)}, u32[]{:S(2)}) %collective-permute-start.8) | collective-permute-done | bytes 258080 | tf_op jit(solution)/shard_map/ppermute | solution.py:21
  48.7 3.5 %all-to-all-start.1 = ((bf16[4,192,896]{2,1,0:T(8,128)(2,1)}), bf16[4,192,896]{2,1,0:T(8,128)(2,1)S(1)}, u32[]{:S(2)}, u32[]{:S(2)}) async-start(bf16[4,192,896]{2,1,0:T(8,128)(2,1)} %get-tuple-element.59), calls=%async_computation.1 | async-start | bytes 2752512 | tf_op jit(solution)/shard_map/all_to_all | solution.py:202
  52.3 4.1 %shard_map.67 = bf16[4,2,96,1024]{3,2,1,0:T(8,128)(2,1)S(1)} custom-call(s32[4]{0:T(128)S(1)} %pad_add_fusion.at_ref, bf16[4,192,896]{2,1,0:T(8,128)(2,1)S(1)} %all-to-all-done.rows_ref, bf16[2,896,1024]{2,1,0:T(8,128)(2,1)} %gate_ref.7, bf16[2,896,1024]{2,1,0:T(8,128)(2,1)} %up_ref.7), custom_call_target="tpu_custom_call" | custom-call | flops 22548578304 | bytes 100663296 | tf_op jit(solution)/shard_map/pallas_call | solution.py:247
  56.3 5.0 %collective-permute-start.4 = (bf16[4,2,96,1024]{3,2,1,0:T(8,128)(2,1)S(1)}, bf16[4,2,96,1024]{3,2,1,0:T(8,128)(2,1)S(1)}, u32[]{:S(2)}, u32[]{:S(2)}) collective-permute-start(bf16[4,2,96,1024]{3,2,1,0:T(8,128)(2,1)S(1)} %shard_map.67), channel_id=1, source_target_pairs={{0,32},{32,0},{64,96},{96,64},{128,160},{160,128},{192,224},{224,1... | collective-permute-start | bytes 4718600 | tf_op jit(solution)/shard_map/ppermute | solution.py:30
  61.3 4.1 %shard_map.66.keep_ref = bf16[4,2,96,1024]{3,2,1,0:T(8,128)(2,1)S(1)} custom-call(s32[4]{0:T(128)S(1)} %pad_add_fusion.at_ref, bf16[4,192,896]{2,1,0:T(8,128)(2,1)S(1)} %all-to-all-done.rows_ref, bf16[2,896,1024]{2,1,0:T(8,128)(2,1)} %gate_ref.7, bf16[2,896,1024]{2,1,0:T(8,128)(2,1)} %up_ref.7), custom_call_target="tpu_custom_call" | custom-call | flops 22548578304 | bytes 100663296 | tf_op jit(solution)/shard_map/pallas_call | solution.py:247
  71.6 4.1 %shard_map.71 = bf16[4,2,96,1024]{3,2,1,0:T(8,128)(2,1)S(1)} custom-call(s32[4]{0:T(128)S(1)} %pad_add_fusion.at_ref, bf16[4,192,896]{2,1,0:T(8,128)(2,1)S(1)} %all-to-all-done.1.rows_ref, bf16[2,896,1024]{2,1,0:T(8,128)(2,1)} %gate_ref.7, bf16[2,896,1024]{2,1,0:T(8,128)(2,1)} %up_ref.7), custom_call_target="tpu_custom_call" | custom-call | flops 22548578304 | bytes 100663296 | tf_op jit(solution)/shard_map/pallas_call | solution.py:247
  76.6 4.1 %shard_map.70.refs_4_ = bf16[4,2,96,1024]{3,2,1,0:T(8,128)(2,1)S(1)} custom-call(s32[4]{0:T(128)S(1)} %pad_add_fusion.at_ref, bf16[4,192,896]{2,1,0:T(8,128)(2,1)S(1)} %all-to-all-done.1.rows_ref, bf16[2,896,1024]{2,1,0:T(8,128)(2,1)} %gate_ref.7, bf16[2,896,1024]{2,1,0:T(8,128)(2,1)} %up_ref.7), custom_call_target="tpu_custom_call" | custom-call | flops 22548578304 | bytes 100663296 | tf_op jit(solution)/shard_map/pallas_call | solution.py:247
  80.7 7.8 %collective-permute-done.6.refs_2_ = bf16[2,96,1024]{2,1,0:T(8,128)(2,1)S(1)} collective-permute-done((bf16[2,96,1024]{2,1,0:T(8,128)(2,1)}, bf16[2,96,1024]{2,1,0:T(8,128)(2,1)S(1)}, u32[]{:S(2)}, u32[]{:S(2)}) %collective-permute-start.6) | collective-permute-done | bytes 393248 | tf_op jit(solution)/shard_map/ppermute | solution.py:30
  93.2 11.2 %collective-permute-done.12.refs_1_ = bf16[3,96,1024]{2,1,0:T(8,128)(2,1)S(1)} collective-permute-done((bf16[3,96,1024]{2,1,0:T(8,128)(2,1)S(1)}, bf16[3,96,1024]{2,1,0:T(8,128)(2,1)S(1)}, u32[]{:S(2)}, u32[]{:S(2)}) %collective-permute-start.12) | collective-permute-done | bytes 589856 | tf_op jit(solution)/shard_map/ppermute | solution.py:30
  104.4 13.6 %collective-permute-done.13.refs_2_ = bf16[3,96,1024]{2,1,0:T(8,128)(2,1)S(1)} collective-permute-done((bf16[3,96,1024]{2,1,0:T(8,128)(2,1)S(1)}, bf16[3,96,1024]{2,1,0:T(8,128)(2,1)S(1)}, u32[]{:S(2)}, u32[]{:S(2)}) %collective-permute-start.13) | collective-permute-done | bytes 589856 | tf_op jit(solution)/shard_map/ppermute | solution.py:30
  123.0 4.1 %shard_map.74 = (bf16[2,96,896]{2,1,0:T(8,128)(2,1)S(1)}, bf16[2,96,896]{2,1,0:T(8,128)(2,1)S(1)}, bf16[2,96,896]{2,1,0:T(8,128)(2,1)S(1)}, bf16[2,96,896]{2,1,0:T(8,128)(2,1)S(1)}) custom-call(s32[4]{0:T(128)S(1)} %pad_add_fusion.at_ref, bf16[4,96,1024]{2,1,0:T(8,128)(2,1)S(1)} %pad_maximum_fusion.own_ref, ...), custom_call_target="tpu_custom_call" | custom-call | bytes 16384 | tf_op jit(solution)/shard_map/pallas_call | solution.py:267
  130.6 4.2 %collective-permute-done.23 = bf16[96,1024]{1,0:T(8,128)(2,1)S(1)} collective-permute-done((bf16[96,1024]{1,0:T(8,128)(2,1)S(1)}, bf16[96,1024]{1,0:T(8,128)(2,1)S(1)}, u32[]{:S(2)}, u32[]{:S(2)}) %collective-permute-start.23) | collective-permute-done | bytes 196640 | tf_op jit(solution)/shard_map/ppermute | solution.py:30
  140.7 4.1 %shard_map.76 = (bf16[2,96,896]{2,1,0:T(8,128)(2,1)S(1)}, bf16[2,96,896]{2,1,0:T(8,128)(2,1)S(1)}, bf16[2,96,896]{2,1,0:T(8,128)(2,1)S(1)}, bf16[2,96,896]{2,1,0:T(8,128)(2,1)S(1)}) custom-call(s32[4]{0:T(128)S(1)} %pad_add_fusion.at_ref, bf16[4,96,1024]{2,1,0:T(8,128)(2,1)S(1)} %pad_maximum_fusion.1.own_ref, ...), custom_call_target="tpu_custom_call" | custom-call | bytes 16384 | tf_op jit(solution)/shard_map/pallas_call | solution.py:267
  148.0 7.1 %collective-permute-done.17.refs_2_ = bf16[2,96,896]{2,1,0:T(8,128)(2,1)S(1)} collective-permute-done((bf16[2,96,896]{2,1,0:T(8,128)(2,1)S(1)}, bf16[2,96,896]{2,1,0:T(8,128)(2,1)S(1)}, u32[]{:S(2)}, u32[]{:S(2)}) %collective-permute-start.17) | collective-permute-done | bytes 344096 | tf_op jit(solution)/shard_map/ppermute | solution.py:21
  158.2 4.9 %collective-permute-done.27.refs_1_ = bf16[2,96,896]{2,1,0:T(8,128)(2,1)S(1)} collective-permute-done((bf16[2,96,896]{2,1,0:T(8,128)(2,1)S(1)}, bf16[2,96,896]{2,1,0:T(8,128)(2,1)S(1)}, u32[]{:S(2)}, u32[]{:S(2)}) %collective-permute-start.27) | collective-permute-done | bytes 344096 | tf_op jit(solution)/shard_map/ppermute | solution.py:21
  163.1 6.7 %collective-permute-done.28.refs_2_ = bf16[2,96,896]{2,1,0:T(8,128)(2,1)S(1)} collective-permute-done((bf16[2,96,896]{2,1,0:T(8,128)(2,1)S(1)}, bf16[2,96,896]{2,1,0:T(8,128)(2,1)S(1)}, u32[]{:S(2)}, u32[]{:S(2)}) %collective-permute-start.28) | collective-permute-done | bytes 344096 | tf_op jit(solution)/shard_map/ppermute | solution.py:21
  171.4 3.7 %collective-permute-start.30 = (bf16[128,896]{1,0:T(8,128)(2,1)S(1)}, bf16[128,896]{1,0:T(8,128)(2,1)S(1)}, u32[]{:S(2)}, u32[]{:S(2)}) collective-permute-start(bf16[128,896]{1,0:T(8,128)(2,1)S(1)} %get-tuple-element.88), channel_id=1, source_target_pairs={{0,16},{1,17},{2,18},{3,19},{4,20},{5,21},{6,22},{7,23},{8,24},{9,... | collective-permute-start | bytes 688136 | tf_op jit(solution)/shard_map/ppermute | solution.py:21
  181.9 6.7 %collective-permute-done.30 = bf16[128,896]{1,0:T(8,128)(2,1)S(1)} collective-permute-done((bf16[128,896]{1,0:T(8,128)(2,1)S(1)}, bf16[128,896]{1,0:T(8,128)(2,1)S(1)}, u32[]{:S(2)}, u32[]{:S(2)}) %collective-permute-start.30) | collective-permute-done | bytes 229408 | tf_op jit(solution)/shard_map/ppermute | solution.py:21
  188.6 9.1 %collective-permute-done.31 = bf16[128,896]{1,0:T(8,128)(2,1)S(1)} collective-permute-done((bf16[128,896]{1,0:T(8,128)(2,1)S(1)}, bf16[128,896]{1,0:T(8,128)(2,1)S(1)}, u32[]{:S(2)}, u32[]{:S(2)}) %collective-permute-start.31) | collective-permute-done | bytes 229408 | tf_op jit(solution)/shard_map/ppermute | solution.py:21
  197.7 9.9 %collective-permute-done.32 = bf16[128,896]{1,0:T(8,128)(2,1)S(1)} collective-permute-done((bf16[128,896]{1,0:T(8,128)(2,1)S(1)}, bf16[128,896]{1,0:T(8,128)(2,1)S(1)}, u32[]{:S(2)}, u32[]{:S(2)}) %collective-permute-start.32) | collective-permute-done | bytes 229408 | tf_op jit(solution)/shard_map/ppermute | solution.py:21
  (68 shorter events, 65.2 us)
Async XLA Ops:
  25.6 14.5 %collective-permute-start.8 = (bf16[144,896]{1,0:T(8,128)(2,1)S(1)}, bf16[144,896]{1,0:T(8,128)(2,1)S(1)}, u32[]{:S(2)}, u32[]{:S(2)}) collective-permute-start(bf16[144,896]{1,0:T(8,128)(2,1)S(1)} %shard_map.64.refs_0_), channel_id=1, source_target_pairs={{0,16},{1,17},{2,18},{3,19},{4,20},{5,21},{6,22},{7,23},{8,24},{9,... | collective-permute-start | bytes 774152 | tf_op jit(solution)/shard_map/ppermute | solution.py:21
  27.4 16.0 %collective-permute-start.9 = (bf16[144,896]{1,0:T(8,128)(2,1)S(1)}, bf16[144,896]{1,0:T(8,128)(2,1)S(1)}, u32[]{:S(2)}, u32[]{:S(2)}) collective-permute-start(bf16[144,896]{1,0:T(8,128)(2,1)S(1)} %collective-permute-done.1.refs_2_), channel_id=1, source_target_pairs={{0,4},{1,5},{2,6},{3,7},{4,8},{5,9},{6,10},{7,11},{8,12},{9,13},{1... | collective-permute-start | bytes 774152 | tf_op jit(solution)/shard_map/ppermute | solution.py:21
  27.4 16.0 %collective-permute-start.10 = (bf16[144,896]{1,0:T(8,128)(2,1)S(1)}, bf16[144,896]{1,0:T(8,128)(2,1)S(1)}, u32[]{:S(2)}, u32[]{:S(2)}) collective-permute-start(bf16[144,896]{1,0:T(8,128)(2,1)S(1)} %collective-permute-done.3.refs_3_), channel_id=1, source_target_pairs={{0,28},{1,29},{2,30},{3,31},{4,0},{5,1},{6,2},{7,3},{8,4},{9,5},{1... | collective-permute-start | bytes 774152 | tf_op jit(solution)/shard_map/ppermute | solution.py:21
  30.0 18.7 %all-to-all-start = ((bf16[4,192,896]{2,1,0:T(8,128)(2,1)}), bf16[4,192,896]{2,1,0:T(8,128)(2,1)S(1)}, u32[]{:S(2)}, u32[]{:S(2)}) async-start(bf16[4,192,896]{2,1,0:T(8,128)(2,1)} %get-tuple-element.51), calls=%async_computation | async-start | bytes 2752512 | tf_op jit(solution)/shard_map/all_to_all | solution.py:202
  48.7 22.9 %all-to-all-start.1 = ((bf16[4,192,896]{2,1,0:T(8,128)(2,1)}), bf16[4,192,896]{2,1,0:T(8,128)(2,1)S(1)}, u32[]{:S(2)}, u32[]{:S(2)}) async-start(bf16[4,192,896]{2,1,0:T(8,128)(2,1)} %get-tuple-element.59), calls=%async_computation.1 | async-start | bytes 2752512 | tf_op jit(solution)/shard_map/all_to_all | solution.py:202
  66.6 14.1 %collective-permute-start.5 = (bf16[2,96,1024]{2,1,0:T(8,128)(2,1)}, bf16[2,96,1024]{2,1,0:T(8,128)(2,1)S(1)}, u32[]{:S(2)}, u32[]{:S(2)}) collective-permute-start(bf16[2,96,1024]{2,1,0:T(8,128)(2,1)} %get-tuple-element.53), channel_id=1, source_target_pairs={{0,64},{32,96},{64,128},{96,160},{128,192},{160,224},{192,0},{224,... | collective-permute-start | bytes 1179656 | tf_op jit(solution)/shard_map/ppermute | solution.py:30
  67.9 20.5 %collective-permute-start.6 = (bf16[2,96,1024]{2,1,0:T(8,128)(2,1)}, bf16[2,96,1024]{2,1,0:T(8,128)(2,1)S(1)}, u32[]{:S(2)}, u32[]{:S(2)}) collective-permute-start(bf16[2,96,1024]{2,1,0:T(8,128)(2,1)} %get-tuple-element.54), channel_id=1, source_target_pairs={{0,128},{32,160},{64,192},{96,224},{128,0},{160,32},{192,64},{224,... | collective-permute-start | bytes 1179656 | tf_op jit(solution)/shard_map/ppermute | solution.py:30
  70.5 17.9 %collective-permute-start.7 = (bf16[2,96,1024]{2,1,0:T(8,128)(2,1)S(1)}, bf16[2,96,1024]{2,1,0:T(8,128)(2,1)S(1)}, u32[]{:S(2)}, u32[]{:S(2)}) collective-permute-start(bf16[2,96,1024]{2,1,0:T(8,128)(2,1)S(1)} %get-tuple-element.55), channel_id=1, source_target_pairs={{0,192},{32,224},{64,0},{96,32},{128,64},{160,96},{192,128},{224,1... | collective-permute-start | bytes 1179656 | tf_op jit(solution)/shard_map/ppermute | solution.py:30
  75.6 12.8 %collective-permute-start.11 = (bf16[4,2,96,1024]{3,2,1,0:T(8,128)(2,1)S(1)}, bf16[4,2,96,1024]{3,2,1,0:T(8,128)(2,1)S(1)}, u32[]{:S(2)}, u32[]{:S(2)}) collective-permute-start(bf16[4,2,96,1024]{3,2,1,0:T(8,128)(2,1)S(1)} %shard_map.71), channel_id=1, source_target_pairs={{0,32},{32,0},{64,96},{96,64},{128,160},{160,128},{192,224},{224,1... | collective-permute-start | bytes 4718600 | tf_op jit(solution)/shard_map/ppermute | solution.py:30
  89.0 15.3 %collective-permute-start.12 = (bf16[3,96,1024]{2,1,0:T(8,128)(2,1)S(1)}, bf16[3,96,1024]{2,1,0:T(8,128)(2,1)S(1)}, u32[]{:S(2)}, u32[]{:S(2)}) collective-permute-start(bf16[3,96,1024]{2,1,0:T(8,128)(2,1)S(1)} %get-tuple-element.62), channel_id=1, source_target_pairs={{0,64},{32,96},{64,128},{96,160},{128,192},{160,224},{192,0},{224,... | collective-permute-start | bytes 1769480 | tf_op jit(solution)/shard_map/ppermute | solution.py:30
  89.2 28.8 %collective-permute-start.13 = (bf16[3,96,1024]{2,1,0:T(8,128)(2,1)S(1)}, bf16[3,96,1024]{2,1,0:T(8,128)(2,1)S(1)}, u32[]{:S(2)}, u32[]{:S(2)}) collective-permute-start(bf16[3,96,1024]{2,1,0:T(8,128)(2,1)S(1)} %get-tuple-element.63), channel_id=1, source_target_pairs={{0,128},{32,160},{64,192},{96,224},{128,0},{160,32},{192,64},{224,... | collective-permute-start | bytes 1769480 | tf_op jit(solution)/shard_map/ppermute | solution.py:30
  92.4 25.6 %collective-permute-start.14 = (bf16[3,96,1024]{2,1,0:T(8,128)(2,1)S(1)}, bf16[3,96,1024]{2,1,0:T(8,128)(2,1)S(1)}, u32[]{:S(2)}, u32[]{:S(2)}) collective-permute-start(bf16[3,96,1024]{2,1,0:T(8,128)(2,1)S(1)} %get-tuple-element.64), channel_id=1, source_target_pairs={{0,192},{32,224},{64,0},{96,32},{128,64},{160,96},{192,128},{224,1... | collective-permute-start | bytes 1769480 | tf_op jit(solution)/shard_map/ppermute | solution.py:30
  137.2 18.0 %collective-permute-start.17 = (bf16[2,96,896]{2,1,0:T(8,128)(2,1)S(1)}, bf16[2,96,896]{2,1,0:T(8,128)(2,1)S(1)}, u32[]{:S(2)}, u32[]{:S(2)}) collective-permute-start(bf16[2,96,896]{2,1,0:T(8,128)(2,1)S(1)} %get-tuple-element.68), channel_id=1, source_target_pairs={{0,2},{1,3},{2,0},{3,1},{4,6},{5,7},{6,4},{7,5},{8,10},{9,11},{10,... | collective-permute-start | bytes 1032200 | tf_op jit(solution)/shard_map/ppermute | solution.py:21
  139.5 15.6 %collective-permute-start.18 = (bf16[2,96,896]{2,1,0:T(8,128)(2,1)S(1)}, bf16[2,96,896]{2,1,0:T(8,128)(2,1)S(1)}, u32[]{:S(2)}, u32[]{:S(2)}) collective-permute-start(bf16[2,96,896]{2,1,0:T(8,128)(2,1)S(1)} %get-tuple-element.69), channel_id=1, source_target_pairs={{0,3},{1,0},{2,1},{3,2},{4,7},{5,4},{6,5},{7,6},{8,11},{9,8},{10,9... | collective-permute-start | bytes 1032200 | tf_op jit(solution)/shard_map/ppermute | solution.py:21
  144.8 18.3 %collective-permute-start.27 = (bf16[2,96,896]{2,1,0:T(8,128)(2,1)S(1)}, bf16[2,96,896]{2,1,0:T(8,128)(2,1)S(1)}, u32[]{:S(2)}, u32[]{:S(2)}) collective-permute-start(bf16[2,96,896]{2,1,0:T(8,128)(2,1)S(1)} %get-tuple-element.82), channel_id=1, source_target_pairs={{0,1},{1,2},{2,3},{3,0},{4,5},{5,6},{6,7},{7,4},{8,9},{9,10},{10,1... | collective-permute-start | bytes 1032200 | tf_op jit(solution)/shard_map/ppermute | solution.py:21
  145.2 24.7 %collective-permute-start.28 = (bf16[2,96,896]{2,1,0:T(8,128)(2,1)S(1)}, bf16[2,96,896]{2,1,0:T(8,128)(2,1)S(1)}, u32[]{:S(2)}, u32[]{:S(2)}) collective-permute-start(bf16[2,96,896]{2,1,0:T(8,128)(2,1)S(1)} %get-tuple-element.83), channel_id=1, source_target_pairs={{0,2},{1,3},{2,0},{3,1},{4,6},{5,7},{6,4},{7,5},{8,10},{9,11},{10,... | collective-permute-start | bytes 1032200 | tf_op jit(solution)/shard_map/ppermute | solution.py:21
  146.7 23.2 %collective-permute-start.29 = (bf16[2,96,896]{2,1,0:T(8,128)(2,1)S(1)}, bf16[2,96,896]{2,1,0:T(8,128)(2,1)S(1)}, u32[]{:S(2)}, u32[]{:S(2)}) collective-permute-start(bf16[2,96,896]{2,1,0:T(8,128)(2,1)S(1)} %get-tuple-element.84), channel_id=1, source_target_pairs={{0,3},{1,0},{2,1},{3,2},{4,7},{5,4},{6,5},{7,6},{8,11},{9,8},{10,9... | collective-permute-start | bytes 1032200 | tf_op jit(solution)/shard_map/ppermute | solution.py:21
  156.7 18.5 %collective-permute-start.19 = (bf16[128,896]{1,0:T(8,128)(2,1)S(1)}, bf16[128,896]{1,0:T(8,128)(2,1)S(1)}, u32[]{:S(2)}, u32[]{:S(2)}) collective-permute-start(bf16[128,896]{1,0:T(8,128)(2,1)S(1)} %get-tuple-element.72), channel_id=1, source_target_pairs={{0,28},{1,29},{2,30},{3,31},{4,0},{5,1},{6,2},{7,3},{8,4},{9,5},{1... | collective-permute-start | bytes 688136 | tf_op jit(solution)/shard_map/ppermute | solution.py:21
  156.8 20.5 %collective-permute-start.20 = (bf16[128,896]{1,0:T(8,128)(2,1)S(1)}, bf16[128,896]{1,0:T(8,128)(2,1)S(1)}, u32[]{:S(2)}, u32[]{:S(2)}) collective-permute-start(bf16[128,896]{1,0:T(8,128)(2,1)S(1)} %get-tuple-element.73), channel_id=1, source_target_pairs={{0,4},{1,5},{2,6},{3,7},{4,8},{5,9},{6,10},{7,11},{8,12},{9,13},{1... | collective-permute-start | bytes 688136 | tf_op jit(solution)/shard_map/ppermute | solution.py:21
  163.1 15.3 %collective-permute-start.21 = (bf16[128,896]{1,0:T(8,128)(2,1)S(1)}, bf16[128,896]{1,0:T(8,128)(2,1)S(1)}, u32[]{:S(2)}, u32[]{:S(2)}) collective-permute-start(bf16[128,896]{1,0:T(8,128)(2,1)S(1)} %get-tuple-element.74), channel_id=1, source_target_pairs={{0,24},{1,25},{2,26},{3,27},{4,28},{5,29},{6,30},{7,31},{8,0},{9,1... | collective-permute-start | bytes 688136 | tf_op jit(solution)/shard_map/ppermute | solution.py:21
  169.9 12.1 %collective-permute-start.22 = (bf16[128,896]{1,0:T(8,128)(2,1)S(1)}, bf16[128,896]{1,0:T(8,128)(2,1)S(1)}, u32[]{:S(2)}, u32[]{:S(2)}) collective-permute-start(bf16[128,896]{1,0:T(8,128)(2,1)S(1)} %get-tuple-element.75), channel_id=1, source_target_pairs={{0,8},{1,9},{2,10},{3,11},{4,12},{5,13},{6,14},{7,15},{8,16},{9,17... | collective-permute-start | bytes 688136 | tf_op jit(solution)/shard_map/ppermute | solution.py:21
  171.4 17.2 %collective-permute-start.30 = (bf16[128,896]{1,0:T(8,128)(2,1)S(1)}, bf16[128,896]{1,0:T(8,128)(2,1)S(1)}, u32[]{:S(2)}, u32[]{:S(2)}) collective-permute-start(bf16[128,896]{1,0:T(8,128)(2,1)S(1)} %get-tuple-element.88), channel_id=1, source_target_pairs={{0,16},{1,17},{2,18},{3,19},{4,20},{5,21},{6,22},{7,23},{8,24},{9,... | collective-permute-start | bytes 688136 | tf_op jit(solution)/shard_map/ppermute | solution.py:21
  175.1 22.6 %collective-permute-start.31 = (bf16[128,896]{1,0:T(8,128)(2,1)S(1)}, bf16[128,896]{1,0:T(8,128)(2,1)S(1)}, u32[]{:S(2)}, u32[]{:S(2)}) collective-permute-start(bf16[128,896]{1,0:T(8,128)(2,1)S(1)} %get-tuple-element.89), channel_id=1, source_target_pairs={{0,20},{1,21},{2,22},{3,23},{4,24},{5,25},{6,26},{7,27},{8,28},{9,... | collective-permute-start | bytes 688136 | tf_op jit(solution)/shard_map/ppermute | solution.py:21
  177.2 30.4 %collective-permute-start.32 = (bf16[128,896]{1,0:T(8,128)(2,1)S(1)}, bf16[128,896]{1,0:T(8,128)(2,1)S(1)}, u32[]{:S(2)}, u32[]{:S(2)}) collective-permute-start(bf16[128,896]{1,0:T(8,128)(2,1)S(1)} %get-tuple-element.90), channel_id=1, source_target_pairs={{0,12},{1,13},{2,14},{3,15},{4,16},{5,17},{6,18},{7,19},{8,20},{9,... | collective-permute-start | bytes 688136 | tf_op jit(solution)/shard_map/ppermute | solution.py:21
  (11 other events, 96.1 us)

commit v2 on v1

--- a/solution.py
+++ b/solution.py
@@ -108,12 +108,14 @@
             (gate_ref, up_ref)[part].at[expert, :, pl.ds(c * half, half)], w_ref.at[n], sems.at[n]
         )
 
-    for n in range(4):
-        fetch(n).start()
+    fetch(0).start()
+    fetch(1).start()
     for r in range(4):
         x_ref[pl.ds(r * held, held), :] = rows_ref[r, pl.ds(pl.multiple_of(expert * held, held), held), :]
     for n, (part, c) in enumerate(pieces):
         fetch(n).wait()
+        if n < 2:
+            fetch(n + 2).start()
         sums = jnp.dot(x_ref[...], w_ref[n], preferred_element_type=F32).astype(BF16)
         for r in range(4):
             out_ref[(r + 4 - y) % 4, part, :, pl.ds(c * half, half)] = sums[
@@ -148,31 +150,44 @@
 
 
 def down_kernel(held, at_ref, own_ref, other_ref, down_ref, *refs):
-    outs, (h_ref, w_ref, sems) = refs[:4], refs[4:]
-    core, y, x = at_ref[1], at_ref[2], at_ref[3]
-
-    def fetch(n):
-        return pltpu.make_async_copy(down_ref.at[(core + n) % 2], w_ref.at[n], sems.at[n])
-
-    for n in range(2):
-        fetch(n).start()
+    apart = len(refs) == 7
+    outs = refs[:4] if apart else [refs[0].at[d] for d in range(4)]
+    h_ref, w_ref, sems = refs[-3:]
+    core, y = at_ref[1], at_ref[2]
+    x = at_ref[3] if apart else 0
+    width = down_ref.shape[2]
+    cuts = [pl.ds(0, 512), pl.ds(512, width - 512)]
+    pieces = [(n, c) for n in range(2) for c in range(2)]
+
+    def fetch(k):
+        n, c = pieces[k]
+        return pltpu.make_async_copy(
+            down_ref.at[(core + n) % 2, :, cuts[c]], w_ref.at[n, :, cuts[c]], sems.at[k]
+        )
+
+    fetch(0).start()
+    fetch(1).start()
     for n, parts_ref in enumerate((own_ref, other_ref)):
         for d in range(4):
-            h_ref[pl.ds(d * held, held), :] = parts_ref[(y + 8 - x - d) % 4]
-        fetch(n).wait()
-        got = jnp.dot(h_ref[...], w_ref[n], preferred_element_type=F32).astype(BF16)
+            h_ref[n, pl.ds(d * held, held), :] = parts_ref[(y + 8 - x - d) % 4]
+    for k, (n, c) in enumerate(pieces):
+        fetch(k).wait()
+        if k < 2:
+            fetch(k + 2).start()
+        got = jnp.dot(h_ref[n], w_ref[n, :, cuts[c]], preferred_element_type=F32).astype(BF16)
         for d in range(4):
-            outs[d][(core + n) % 2] = got[d * held : (d + 1) * held]
-
-
-def mix_kernel(held, rows, at_ref, *refs):
-    backs, (code_ref, weight_ref), outs = refs[:4], refs[4:6], refs[6:]
+            outs[d][(core + n) % 2, :, cuts[c]] = got[d * held : (d + 1) * held]
+
+
+def mix_kernel(held, rows, apart, at_ref, *refs):
+    backs, refs = (refs[:4], refs[4:]) if apart else ([refs[0].at[d] for d in range(4)], refs[1:])
+    (code_ref, weight_ref), outs = refs[:2], refs[2:]
     width = code_ref.shape[1]
     at = lax.broadcasted_iota(jnp.int32, (held, width), 0).astype(F32)
     share = []
     for d in range(4):
         for e in range(2):
-            j = pl.ds((at_ref[3] + 4 - d) % 4 * 2 + e, 1)
+            j = pl.ds((at_ref[3] + 4 - d) % 4 * 2 + e, 1) if apart else pl.ds(2 * d + e, 1)
             share.append(jnp.where(at == code_ref[j, :], weight_ref[j, :], 0.0))
     back = jnp.concatenate([backs[d][e] for d in range(4) for e in range(2)], axis=0)
     total = lax.dot_general(
@@ -263,25 +278,24 @@
     def spread(values):
         return [along_section(v, q, 0) if q else v for q, v in enumerate(values)]
 
-    def contract(parts, others):
-        out = call(
+    def contract(parts, others, apart):
+        return call(
             functools.partial(down_kernel, held),
-            [shape(2, held, width)] * 4,
+            [shape(2, held, width)] * 4 if apart else [shape(4, 2, held, width)],
             [SMEM, VMEM, VMEM, HBM],
             scratch=[
-                pltpu.VMEM((4 * held, units), BF16),
+                pltpu.VMEM((2, 4 * held, units), BF16),
                 pltpu.VMEM((2, units, width), BF16),
-                pltpu.SemaphoreType.DMA((2,)),
+                pltpu.SemaphoreType.DMA((4,)),
             ],
             moved=1 << 10,
         )(at, parts, others, down_weight)
-        return out, [along_expert(v, 0, d) if d else v for d, v in enumerate(out)]
 
     def mix(chunk, back, code, weight):
         mixed = call(
-            functools.partial(mix_kernel, held, rows),
+            functools.partial(mix_kernel, held, rows, len(back) == 4),
             [shape(rows, width)] * len(chunk),
-            [SMEM] + [VMEM] * 6,
+            [SMEM] + [VMEM] * (len(back) + 2),
             flops=16 * held * len(chunk) * rows * width,
             moved=2 << 20,
         )(at, *back, code, weight)
@@ -304,11 +318,13 @@
     hidden = call(silu_kernel, shape(held, units), [VMEM] * 4, moved=1 << 20)(*mail)
     parts, hidden = lax.optimization_barrier((parts, hidden))
     pieces = spread([hidden] * 4)
-    out, back = contract(parts, others)
+    out = contract(parts, others, False)
+    back = [swap_x(out[0])]
     pieces, out = lax.optimization_barrier((pieces, out))
     parts = jnp.stack(pieces)
     others = along_section(parts, 0, 1)
-    _, back_second = contract(parts, others)
+    out_second = contract(parts, others, True)
+    back_second = [along_expert(v, 0, d) if d else v for d, v in enumerate(out_second)]
     partials = mix(near, back, *first_codes) + mix(far, back_second, *second_codes)
     return sum(p.astype(F32) for p in partials).astype(BF16)
 

time: 209 us -> 205 us (0.981)
  waiting for transfers between devices: 113 us -> 103 us
  Pallas kernels: 36 us -> 38.7 us
  starting transfers between devices: 58.5 us -> 60.7 us
    ppermute x20 -> x17, waiting for transfers between devices: 69.7 us -> 62 us  [along_expert(): lax.ppermute(value, 'expert', [(i, (i // NX + dz) % planes * NX + (i % NX...]
    all_to_all x2 -> x3, starting transfers between devices: 7.56 us -> 12 us  [swap_x(): lax.all_to_all(value, 'expert', 0, 0, axis_index_groups=x_groups, tiled=T...]
    ppermute x13, waiting for transfers between devices: 40.2 us -> 36.1 us  [along_section(): lax.ppermute(value, 'section', [(i, (i + CORES * dy) % count ^ flip) for...]
    all_to_all x2 -> x3, waiting for transfers between devices: 2.6 us -> 5.3 us  [swap_x(): lax.all_to_all(value, 'expert', 0, 0, axis_index_groups=x_groups, tiled=T...]
    ppermute x20 -> x17, starting transfers between devices: 30.7 us -> 28.2 us  [along_expert(): lax.ppermute(value, 'expert', [(i, (i // NX + dz) % planes * NX + (i % NX...]
    pallas_call x4, Pallas kernels: 11.3 us -> 13.5 us  [the longest x2 10.4 us: contract(): call(functools.partial(down_kernel, held), [shape(2, held, width)] * 4 if...]
  transfers between devices with their start and end apart: 35 -> 33, of which waited for: 19 -> 18; matrix products, arithmetic and copies ran while one was open for 0% -> 0% of each run, Pallas kernels for 15% -> 17%
where the time goes in v2:
time: 205 us; the launch traced here: 204 us
  waiting for transfers between devices  103 us (50%)
  starting transfers between devices  60.7 us (30%)
  Pallas kernels  38.7 us (19%)
    ppermute x17, waiting for transfers between devices, along_expert(): lax.ppermute(value, 'expert', [(i, (i // NX + dz) % planes * NX + (i % NX...  62 us
    ppermute x13, waiting for transfers between devices, along_section(): lax.ppermute(value, 'section', [(i, (i + CORES * dy) % count ^ flip) for...  36.1 us
    ppermute x17, starting transfers between devices, along_expert(): lax.ppermute(value, 'expert', [(i, (i // NX + dz) % planes * NX + (i % NX...  28.2 us
    ppermute x13, starting transfers between devices, along_section(): lax.ppermute(value, 'section', [(i, (i + CORES * dy) % count ^ flip) for...  20.4 us
    pallas_call x4, Pallas kernels, expand(): call(functools.partial(up_kernel, held, flip), shape(4, 2, held, units),...  16.6 us
    all_to_all x3, starting transfers between devices, swap_x(): lax.all_to_all(value, 'expert', 0, 0, axis_index_groups=x_groups, tiled=T...  12 us
    pallas_call x2, Pallas kernels, contract(): call(functools.partial(down_kernel, held), [shape(2, held, width)] * 4 if...  10.4 us
    pallas_call x2, Pallas kernels, body(): call(functools.partial(select_kernel, capacity, rows), [shape(4, 2 * held...  5.53 us
  transfers between devices with their start and end apart: 33, of which 18 were waited for; matrix products, arithmetic and copies ran while one was open for 0% of the time, Pallas kernels for 17%

profile of v2, /device:TPU:1, one launch (start us, length us, event | category | flops | bytes accessed | tf_op | source)
XLA Modules:
  0.0 204.3 jit_solution(14647289512838242741)
XLA Ops:
  1.0 6.5 %collective-permute-start.2 = (bf16[144,896]{1,0:T(8,128)(2,1)S(1)}, bf16[144,896]{1,0:T(8,128)(2,1)S(1)}, u32[]{:S(2)}, u32[]{:S(2)}) collective-permute-start(bf16[144,896]{1,0:T(8,128)(2,1)S(1)} %shard_map.64.refs_0_), channel_id=1, source_target_pairs={{0,28},{1,29},{2,30},{3,31},{4,0},{5,1},{6,2},{7,3},{8,4},{9,5},{1... | collective-permute-start | bytes 774152 | tf_op jit(solution)/shard_map/ppermute | solution.py:21
  7.5 4.9 %collective-permute-done.2.refs_1_ = bf16[144,896]{1,0:T(8,128)(2,1)S(1)} collective-permute-done((bf16[144,896]{1,0:T(8,128)(2,1)S(1)}, bf16[144,896]{1,0:T(8,128)(2,1)S(1)}, u32[]{:S(2)}, u32[]{:S(2)}) %collective-permute-start.2) | collective-permute-done | bytes 258080 | tf_op jit(solution)/shard_map/ppermute | solution.py:21
  15.9 3.9 %collective-permute-done.3.refs_3_ = bf16[144,896]{1,0:T(8,128)(2,1)S(1)} collective-permute-done((bf16[144,896]{1,0:T(8,128)(2,1)S(1)}, bf16[144,896]{1,0:T(8,128)(2,1)S(1)}, u32[]{:S(2)}, u32[]{:S(2)}) %collective-permute-start.3) | collective-permute-done | bytes 258080 | tf_op jit(solution)/shard_map/ppermute | solution.py:21
  30.0 4.0 %all-to-all-start = ((bf16[4,192,896]{2,1,0:T(8,128)(2,1)}), bf16[4,192,896]{2,1,0:T(8,128)(2,1)S(1)}, u32[]{:S(2)}, u32[]{:S(2)}) async-start(bf16[4,192,896]{2,1,0:T(8,128)(2,1)} %get-tuple-element.47), calls=%async_computation | async-start | bytes 2752512 | tf_op jit(solution)/shard_map/all_to_all | solution.py:217
  34.0 6.1 %collective-permute-done.8.refs_1_ = bf16[144,896]{1,0:T(8,128)(2,1)S(1)} collective-permute-done((bf16[144,896]{1,0:T(8,128)(2,1)S(1)}, bf16[144,896]{1,0:T(8,128)(2,1)S(1)}, u32[]{:S(2)}, u32[]{:S(2)}) %collective-permute-start.8) | collective-permute-done | bytes 258080 | tf_op jit(solution)/shard_map/ppermute | solution.py:21
  48.7 3.5 %all-to-all-start.1 = ((bf16[4,192,896]{2,1,0:T(8,128)(2,1)}), bf16[4,192,896]{2,1,0:T(8,128)(2,1)S(1)}, u32[]{:S(2)}, u32[]{:S(2)}) async-start(bf16[4,192,896]{2,1,0:T(8,128)(2,1)} %get-tuple-element.55), calls=%async_computation.1 | async-start | bytes 2752512 | tf_op jit(solution)/shard_map/all_to_all | solution.py:217
  52.3 4.2 %shard_map.67 = bf16[4,2,96,1024]{3,2,1,0:T(8,128)(2,1)S(1)} custom-call(s32[4]{0:T(128)S(1)} %pad_add_fusion.at_ref, bf16[4,192,896]{2,1,0:T(8,128)(2,1)S(1)} %all-to-all-done.rows_ref, bf16[2,896,1024]{2,1,0:T(8,128)(2,1)} %gate_ref.7, bf16[2,896,1024]{2,1,0:T(8,128)(2,1)} %up_ref.7), custom_call_target="tpu_custom_call" | custom-call | flops 22548578304 | bytes 100663296 | tf_op jit(solution)/shard_map/pallas_call | solution.py:262
  56.4 5.0 %collective-permute-start.4 = (bf16[4,2,96,1024]{3,2,1,0:T(8,128)(2,1)S(1)}, bf16[4,2,96,1024]{3,2,1,0:T(8,128)(2,1)S(1)}, u32[]{:S(2)}, u32[]{:S(2)}) collective-permute-start(bf16[4,2,96,1024]{3,2,1,0:T(8,128)(2,1)S(1)} %shard_map.67), channel_id=1, source_target_pairs={{0,32},{32,0},{64,96},{96,64},{128,160},{160,128},{192,224},{224,1... | collective-permute-start | bytes 4718600 | tf_op jit(solution)/shard_map/ppermute | solution.py:30
  61.4 4.2 %shard_map.66.keep_ref = bf16[4,2,96,1024]{3,2,1,0:T(8,128)(2,1)S(1)} custom-call(s32[4]{0:T(128)S(1)} %pad_add_fusion.at_ref, bf16[4,192,896]{2,1,0:T(8,128)(2,1)S(1)} %all-to-all-done.rows_ref, bf16[2,896,1024]{2,1,0:T(8,128)(2,1)} %gate_ref.7, bf16[2,896,1024]{2,1,0:T(8,128)(2,1)} %up_ref.7), custom_call_target="tpu_custom_call" | custom-call | flops 22548578304 | bytes 100663296 | tf_op jit(solution)/shard_map/pallas_call | solution.py:262
  71.8 4.2 %shard_map.71 = bf16[4,2,96,1024]{3,2,1,0:T(8,128)(2,1)S(1)} custom-call(s32[4]{0:T(128)S(1)} %pad_add_fusion.at_ref, bf16[4,192,896]{2,1,0:T(8,128)(2,1)S(1)} %all-to-all-done.1.rows_ref, bf16[2,896,1024]{2,1,0:T(8,128)(2,1)} %gate_ref.7, bf16[2,896,1024]{2,1,0:T(8,128)(2,1)} %up_ref.7), custom_call_target="tpu_custom_call" | custom-call | flops 22548578304 | bytes 100663296 | tf_op jit(solution)/shard_map/pallas_call | solution.py:262
  76.9 4.2 %shard_map.70.refs_4_ = bf16[4,2,96,1024]{3,2,1,0:T(8,128)(2,1)S(1)} custom-call(s32[4]{0:T(128)S(1)} %pad_add_fusion.at_ref, bf16[4,192,896]{2,1,0:T(8,128)(2,1)S(1)} %all-to-all-done.1.rows_ref, bf16[2,896,1024]{2,1,0:T(8,128)(2,1)} %gate_ref.7, bf16[2,896,1024]{2,1,0:T(8,128)(2,1)} %up_ref.7), custom_call_target="tpu_custom_call" | custom-call | flops 22548578304 | bytes 100663296 | tf_op jit(solution)/shard_map/pallas_call | solution.py:262
  81.0 7.6 %collective-permute-done.6.refs_2_ = bf16[2,96,1024]{2,1,0:T(8,128)(2,1)S(1)} collective-permute-done((bf16[2,96,1024]{2,1,0:T(8,128)(2,1)}, bf16[2,96,1024]{2,1,0:T(8,128)(2,1)S(1)}, u32[]{:S(2)}, u32[]{:S(2)}) %collective-permute-start.6) | collective-permute-done | bytes 393248 | tf_op jit(solution)/shard_map/ppermute | solution.py:30
  93.3 11.2 %collective-permute-done.12.refs_1_ = bf16[3,96,1024]{2,1,0:T(8,128)(2,1)S(1)} collective-permute-done((bf16[3,96,1024]{2,1,0:T(8,128)(2,1)S(1)}, bf16[3,96,1024]{2,1,0:T(8,128)(2,1)S(1)}, u32[]{:S(2)}, u32[]{:S(2)}) %collective-permute-start.12) | collective-permute-done | bytes 589856 | tf_op jit(solution)/shard_map/ppermute | solution.py:30
  104.6 13.6 %collective-permute-done.13.refs_2_ = bf16[3,96,1024]{2,1,0:T(8,128)(2,1)S(1)} collective-permute-done((bf16[3,96,1024]{2,1,0:T(8,128)(2,1)S(1)}, bf16[3,96,1024]{2,1,0:T(8,128)(2,1)S(1)}, u32[]{:S(2)}, u32[]{:S(2)}) %collective-permute-start.13) | collective-permute-done | bytes 589856 | tf_op jit(solution)/shard_map/ppermute | solution.py:30
  123.2 5.4 %shard_map.74 = bf16[4,2,96,896]{3,2,1,0:T(8,128)(2,1)} custom-call(s32[4]{0:T(128)S(1)} %pad_add_fusion.at_ref, bf16[4,96,1024]{2,1,0:T(8,128)(2,1)S(1)} %pad_maximum_fusion.own_ref, bf16[4,96,1024]{2,1,0:T(8,128)(2,1)S(1)} %collective-permute-done.15.other_ref, bf16[2,1024,896]{2,1,0:T(8,128)(2,1)} %down_ref.3), custom_call_target="tpu_custom_call" | custom-call | bytes 16384 | tf_op jit(solution)/shard_map/pallas_call | solution.py:282
  128.5 4.5 %all-to-all-start.2 = ((bf16[4,2,96,896]{3,2,1,0:T(8,128)(2,1)}), bf16[4,2,96,896]{3,2,1,0:T(8,128)(2,1)S(1)}, u32[]{:S(2)}, u32[]{:S(2)}) async-start(bf16[4,2,96,896]{3,2,1,0:T(8,128)(2,1)} %shard_map.74), calls=%async_computation.2 | async-start | bytes 2752512 | tf_op jit(solution)/shard_map/all_to_all | solution.py:217
  137.7 5.0 %shard_map.76 = (bf16[2,96,896]{2,1,0:T(8,128)(2,1)S(1)}, bf16[2,96,896]{2,1,0:T(8,128)(2,1)}, bf16[2,96,896]{2,1,0:T(8,128)(2,1)}, bf16[2,96,896]{2,1,0:T(8,128)(2,1)S(1)}) custom-call(s32[4]{0:T(128)S(1)} %pad_add_fusion.at_ref, bf16[4,96,1024]{2,1,0:T(8,128)(2,1)S(1)} %pad_maximum_fusion.1.own_ref, ...), custom_call_target="tpu_custom_call" | custom-call | bytes 16384 | tf_op jit(solution)/shard_map/pallas_call | solution.py:282
  154.0 6.8 %collective-permute-done.24.refs_1_ = bf16[2,96,896]{2,1,0:T(8,128)(2,1)S(1)} collective-permute-done((bf16[2,96,896]{2,1,0:T(8,128)(2,1)}, bf16[2,96,896]{2,1,0:T(8,128)(2,1)S(1)}, u32[]{:S(2)}, u32[]{:S(2)}) %collective-permute-start.24) | collective-permute-done | bytes 344096 | tf_op jit(solution)/shard_map/ppermute | solution.py:21
  160.8 4.8 %collective-permute-done.25.refs_2_ = bf16[2,96,896]{2,1,0:T(8,128)(2,1)S(1)} collective-permute-done((bf16[2,96,896]{2,1,0:T(8,128)(2,1)}, bf16[2,96,896]{2,1,0:T(8,128)(2,1)S(1)}, u32[]{:S(2)}, u32[]{:S(2)}) %collective-permute-start.25) | collective-permute-done | bytes 344096 | tf_op jit(solution)/shard_map/ppermute | solution.py:21
  167.2 3.7 %collective-permute-start.27 = (bf16[128,896]{1,0:T(8,128)(2,1)S(1)}, bf16[128,896]{1,0:T(8,128)(2,1)S(1)}, u32[]{:S(2)}, u32[]{:S(2)}) collective-permute-start(bf16[128,896]{1,0:T(8,128)(2,1)S(1)} %get-tuple-element.80), channel_id=1, source_target_pairs={{0,16},{1,17},{2,18},{3,19},{4,20},{5,21},{6,22},{7,23},{8,24},{9,... | collective-permute-start | bytes 688136 | tf_op jit(solution)/shard_map/ppermute | solution.py:21
  174.2 3.4 %collective-permute-done.19 = bf16[128,896]{1,0:T(8,128)(2,1)S(1)} collective-permute-done((bf16[128,896]{1,0:T(8,128)(2,1)S(1)}, bf16[128,896]{1,0:T(8,128)(2,1)S(1)}, u32[]{:S(2)}, u32[]{:S(2)}) %collective-permute-start.19) | collective-permute-done | bytes 229408 | tf_op jit(solution)/shard_map/ppermute | solution.py:21
  177.6 7.0 %collective-permute-done.27 = bf16[128,896]{1,0:T(8,128)(2,1)S(1)} collective-permute-done((bf16[128,896]{1,0:T(8,128)(2,1)S(1)}, bf16[128,896]{1,0:T(8,128)(2,1)S(1)}, u32[]{:S(2)}, u32[]{:S(2)}) %collective-permute-start.27) | collective-permute-done | bytes 229408 | tf_op jit(solution)/shard_map/ppermute | solution.py:21
  184.6 8.5 %collective-permute-done.28 = bf16[128,896]{1,0:T(8,128)(2,1)S(1)} collective-permute-done((bf16[128,896]{1,0:T(8,128)(2,1)S(1)}, bf16[128,896]{1,0:T(8,128)(2,1)S(1)}, u32[]{:S(2)}, u32[]{:S(2)}) %collective-permute-start.28) | collective-permute-done | bytes 229408 | tf_op jit(solution)/shard_map/ppermute | solution.py:21
  193.0 10.3 %collective-permute-done.29 = bf16[128,896]{1,0:T(8,128)(2,1)S(1)} collective-permute-done((bf16[128,896]{1,0:T(8,128)(2,1)S(1)}, bf16[128,896]{1,0:T(8,128)(2,1)S(1)}, u32[]{:S(2)}, u32[]{:S(2)}) %collective-permute-start.29) | collective-permute-done | bytes 229408 | tf_op jit(solution)/shard_map/ppermute | solution.py:21
  (64 shorter events, 61.9 us)
Async XLA Ops:
  25.6 14.5 %collective-permute-start.8 = (bf16[144,896]{1,0:T(8,128)(2,1)S(1)}, bf16[144,896]{1,0:T(8,128)(2,1)S(1)}, u32[]{:S(2)}, u32[]{:S(2)}) collective-permute-start(bf16[144,896]{1,0:T(8,128)(2,1)S(1)} %shard_map.64.refs_0_), channel_id=1, source_target_pairs={{0,16},{1,17},{2,18},{3,19},{4,20},{5,21},{6,22},{7,23},{8,24},{9,... | collective-permute-start | bytes 774152 | tf_op jit(solution)/shard_map/ppermute | solution.py:21
  27.4 16.0 %collective-permute-start.9 = (bf16[144,896]{1,0:T(8,128)(2,1)S(1)}, bf16[144,896]{1,0:T(8,128)(2,1)S(1)}, u32[]{:S(2)}, u32[]{:S(2)}) collective-permute-start(bf16[144,896]{1,0:T(8,128)(2,1)S(1)} %collective-permute-done.1.refs_2_), channel_id=1, source_target_pairs={{0,4},{1,5},{2,6},{3,7},{4,8},{5,9},{6,10},{7,11},{8,12},{9,13},{1... | collective-permute-start | bytes 774152 | tf_op jit(solution)/shard_map/ppermute | solution.py:21
  27.4 16.0 %collective-permute-start.10 = (bf16[144,896]{1,0:T(8,128)(2,1)S(1)}, bf16[144,896]{1,0:T(8,128)(2,1)S(1)}, u32[]{:S(2)}, u32[]{:S(2)}) collective-permute-start(bf16[144,896]{1,0:T(8,128)(2,1)S(1)} %collective-permute-done.3.refs_3_), channel_id=1, source_target_pairs={{0,28},{1,29},{2,30},{3,31},{4,0},{5,1},{6,2},{7,3},{8,4},{9,5},{1... | collective-permute-start | bytes 774152 | tf_op jit(solution)/shard_map/ppermute | solution.py:21
  30.0 18.7 %all-to-all-start = ((bf16[4,192,896]{2,1,0:T(8,128)(2,1)}), bf16[4,192,896]{2,1,0:T(8,128)(2,1)S(1)}, u32[]{:S(2)}, u32[]{:S(2)}) async-start(bf16[4,192,896]{2,1,0:T(8,128)(2,1)} %get-tuple-element.47), calls=%async_computation | async-start | bytes 2752512 | tf_op jit(solution)/shard_map/all_to_all | solution.py:217
  48.7 23.0 %all-to-all-start.1 = ((bf16[4,192,896]{2,1,0:T(8,128)(2,1)}), bf16[4,192,896]{2,1,0:T(8,128)(2,1)S(1)}, u32[]{:S(2)}, u32[]{:S(2)}) async-start(bf16[4,192,896]{2,1,0:T(8,128)(2,1)} %get-tuple-element.55), calls=%async_computation.1 | async-start | bytes 2752512 | tf_op jit(solution)/shard_map/all_to_all | solution.py:217
  66.8 14.3 %collective-permute-start.5 = (bf16[2,96,1024]{2,1,0:T(8,128)(2,1)}, bf16[2,96,1024]{2,1,0:T(8,128)(2,1)S(1)}, u32[]{:S(2)}, u32[]{:S(2)}) collective-permute-start(bf16[2,96,1024]{2,1,0:T(8,128)(2,1)} %get-tuple-element.49), channel_id=1, source_target_pairs={{0,64},{32,96},{64,128},{96,160},{128,192},{160,224},{192,0},{224,... | collective-permute-start | bytes 1179656 | tf_op jit(solution)/shard_map/ppermute | solution.py:30
  68.1 20.5 %collective-permute-start.6 = (bf16[2,96,1024]{2,1,0:T(8,128)(2,1)}, bf16[2,96,1024]{2,1,0:T(8,128)(2,1)S(1)}, u32[]{:S(2)}, u32[]{:S(2)}) collective-permute-start(bf16[2,96,1024]{2,1,0:T(8,128)(2,1)} %get-tuple-element.50), channel_id=1, source_target_pairs={{0,128},{32,160},{64,192},{96,224},{128,0},{160,32},{192,64},{224,... | collective-permute-start | bytes 1179656 | tf_op jit(solution)/shard_map/ppermute | solution.py:30
  70.7 17.9 %collective-permute-start.7 = (bf16[2,96,1024]{2,1,0:T(8,128)(2,1)S(1)}, bf16[2,96,1024]{2,1,0:T(8,128)(2,1)S(1)}, u32[]{:S(2)}, u32[]{:S(2)}) collective-permute-start(bf16[2,96,1024]{2,1,0:T(8,128)(2,1)S(1)} %get-tuple-element.51), channel_id=1, source_target_pairs={{0,192},{32,224},{64,0},{96,32},{128,64},{160,96},{192,128},{224,1... | collective-permute-start | bytes 1179656 | tf_op jit(solution)/shard_map/ppermute | solution.py:30
  75.9 12.7 %collective-permute-start.11 = (bf16[4,2,96,1024]{3,2,1,0:T(8,128)(2,1)S(1)}, bf16[4,2,96,1024]{3,2,1,0:T(8,128)(2,1)S(1)}, u32[]{:S(2)}, u32[]{:S(2)}) collective-permute-start(bf16[4,2,96,1024]{3,2,1,0:T(8,128)(2,1)S(1)} %shard_map.71), channel_id=1, source_target_pairs={{0,32},{32,0},{64,96},{96,64},{128,160},{160,128},{192,224},{224,1... | collective-permute-start | bytes 4718600 | tf_op jit(solution)/shard_map/ppermute | solution.py:30
  89.2 15.3 %collective-permute-start.12 = (bf16[3,96,1024]{2,1,0:T(8,128)(2,1)S(1)}, bf16[3,96,1024]{2,1,0:T(8,128)(2,1)S(1)}, u32[]{:S(2)}, u32[]{:S(2)}) collective-permute-start(bf16[3,96,1024]{2,1,0:T(8,128)(2,1)S(1)} %get-tuple-element.58), channel_id=1, source_target_pairs={{0,64},{32,96},{64,128},{96,160},{128,192},{160,224},{192,0},{224,... | collective-permute-start | bytes 1769480 | tf_op jit(solution)/shard_map/ppermute | solution.py:30
  89.4 28.8 %collective-permute-start.13 = (bf16[3,96,1024]{2,1,0:T(8,128)(2,1)S(1)}, bf16[3,96,1024]{2,1,0:T(8,128)(2,1)S(1)}, u32[]{:S(2)}, u32[]{:S(2)}) collective-permute-start(bf16[3,96,1024]{2,1,0:T(8,128)(2,1)S(1)} %get-tuple-element.59), channel_id=1, source_target_pairs={{0,128},{32,160},{64,192},{96,224},{128,0},{160,32},{192,64},{224,... | collective-permute-start | bytes 1769480 | tf_op jit(solution)/shard_map/ppermute | solution.py:30
  92.6 25.6 %collective-permute-start.14 = (bf16[3,96,1024]{2,1,0:T(8,128)(2,1)S(1)}, bf16[3,96,1024]{2,1,0:T(8,128)(2,1)S(1)}, u32[]{:S(2)}, u32[]{:S(2)}) collective-permute-start(bf16[3,96,1024]{2,1,0:T(8,128)(2,1)S(1)} %get-tuple-element.60), channel_id=1, source_target_pairs={{0,192},{32,224},{64,0},{96,32},{128,64},{160,96},{192,128},{224,1... | collective-permute-start | bytes 1769480 | tf_op jit(solution)/shard_map/ppermute | solution.py:30
  120.0 13.1 %collective-permute-start.22 = (bf16[96,1024]{1,0:T(8,128)(2,1)S(1)}, bf16[96,1024]{1,0:T(8,128)(2,1)S(1)}, u32[]{:S(2)}, u32[]{:S(2)}) collective-permute-start(bf16[96,1024]{1,0:T(8,128)(2,1)S(1)} %shard_map.73), channel_id=1, source_target_pairs={{0,192},{32,224},{64,0},{96,32},{128,64},{160,96},{192,128},{224,1... | collective-permute-start | bytes 589832 | tf_op jit(solution)/shard_map/ppermute | solution.py:30
  128.5 22.3 %all-to-all-start.2 = ((bf16[4,2,96,896]{3,2,1,0:T(8,128)(2,1)}), bf16[4,2,96,896]{3,2,1,0:T(8,128)(2,1)S(1)}, u32[]{:S(2)}, u32[]{:S(2)}) async-start(bf16[4,2,96,896]{3,2,1,0:T(8,128)(2,1)} %shard_map.74), calls=%async_computation.2 | async-start | bytes 2752512 | tf_op jit(solution)/shard_map/all_to_all | solution.py:217
  142.8 18.0 %collective-permute-start.24 = (bf16[2,96,896]{2,1,0:T(8,128)(2,1)}, bf16[2,96,896]{2,1,0:T(8,128)(2,1)S(1)}, u32[]{:S(2)}, u32[]{:S(2)}) collective-permute-start(bf16[2,96,896]{2,1,0:T(8,128)(2,1)} %get-tuple-element.74), channel_id=1, source_target_pairs={{0,1},{1,2},{2,3},{3,0},{4,5},{5,6},{6,7},{7,4},{8,9},{9,10},{10,1... | collective-permute-start | bytes 1032200 | tf_op jit(solution)/shard_map/ppermute | solution.py:21
  144.6 21.0 %collective-permute-start.25 = (bf16[2,96,896]{2,1,0:T(8,128)(2,1)}, bf16[2,96,896]{2,1,0:T(8,128)(2,1)S(1)}, u32[]{:S(2)}, u32[]{:S(2)}) collective-permute-start(bf16[2,96,896]{2,1,0:T(8,128)(2,1)} %get-tuple-element.75), channel_id=1, source_target_pairs={{0,2},{1,3},{2,0},{3,1},{4,6},{5,7},{6,4},{7,5},{8,10},{9,11},{10,... | collective-permute-start | bytes 1032200 | tf_op jit(solution)/shard_map/ppermute | solution.py:21
  147.0 18.6 %collective-permute-start.26 = (bf16[2,96,896]{2,1,0:T(8,128)(2,1)S(1)}, bf16[2,96,896]{2,1,0:T(8,128)(2,1)S(1)}, u32[]{:S(2)}, u32[]{:S(2)}) collective-permute-start(bf16[2,96,896]{2,1,0:T(8,128)(2,1)S(1)} %get-tuple-element.76), channel_id=1, source_target_pairs={{0,3},{1,0},{2,1},{3,2},{4,7},{5,4},{6,5},{7,6},{8,11},{9,8},{10,9... | collective-permute-start | bytes 1032200 | tf_op jit(solution)/shard_map/ppermute | solution.py:21
  152.4 18.5 %collective-permute-start.16 = (bf16[128,896]{1,0:T(8,128)(2,1)S(1)}, bf16[128,896]{1,0:T(8,128)(2,1)S(1)}, u32[]{:S(2)}, u32[]{:S(2)}) collective-permute-start(bf16[128,896]{1,0:T(8,128)(2,1)S(1)} %get-tuple-element.64), channel_id=1, source_target_pairs={{0,28},{1,29},{2,30},{3,31},{4,0},{5,1},{6,2},{7,3},{8,4},{9,5},{1... | collective-permute-start | bytes 688136 | tf_op jit(solution)/shard_map/ppermute | solution.py:21
  152.5 20.5 %collective-permute-start.17 = (bf16[128,896]{1,0:T(8,128)(2,1)S(1)}, bf16[128,896]{1,0:T(8,128)(2,1)S(1)}, u32[]{:S(2)}, u32[]{:S(2)}) collective-permute-start(bf16[128,896]{1,0:T(8,128)(2,1)S(1)} %get-tuple-element.65), channel_id=1, source_target_pairs={{0,4},{1,5},{2,6},{3,7},{4,8},{5,9},{6,10},{7,11},{8,12},{9,13},{1... | collective-permute-start | bytes 688136 | tf_op jit(solution)/shard_map/ppermute | solution.py:21
  160.8 13.4 %collective-permute-start.18 = (bf16[128,896]{1,0:T(8,128)(2,1)S(1)}, bf16[128,896]{1,0:T(8,128)(2,1)S(1)}, u32[]{:S(2)}, u32[]{:S(2)}) collective-permute-start(bf16[128,896]{1,0:T(8,128)(2,1)S(1)} %get-tuple-element.66), channel_id=1, source_target_pairs={{0,24},{1,25},{2,26},{3,27},{4,28},{5,29},{6,30},{7,31},{8,0},{9,1... | collective-permute-start | bytes 688136 | tf_op jit(solution)/shard_map/ppermute | solution.py:21
  165.6 12.0 %collective-permute-start.19 = (bf16[128,896]{1,0:T(8,128)(2,1)S(1)}, bf16[128,896]{1,0:T(8,128)(2,1)S(1)}, u32[]{:S(2)}, u32[]{:S(2)}) collective-permute-start(bf16[128,896]{1,0:T(8,128)(2,1)S(1)} %get-tuple-element.67), channel_id=1, source_target_pairs={{0,8},{1,9},{2,10},{3,11},{4,12},{5,13},{6,14},{7,15},{8,16},{9,17... | collective-permute-start | bytes 688136 | tf_op jit(solution)/shard_map/ppermute | solution.py:21
  167.2 17.4 %collective-permute-start.27 = (bf16[128,896]{1,0:T(8,128)(2,1)S(1)}, bf16[128,896]{1,0:T(8,128)(2,1)S(1)}, u32[]{:S(2)}, u32[]{:S(2)}) collective-permute-start(bf16[128,896]{1,0:T(8,128)(2,1)S(1)} %get-tuple-element.80), channel_id=1, source_target_pairs={{0,16},{1,17},{2,18},{3,19},{4,20},{5,21},{6,22},{7,23},{8,24},{9,... | collective-permute-start | bytes 688136 | tf_op jit(solution)/shard_map/ppermute | solution.py:21
  170.9 22.1 %collective-permute-start.28 = (bf16[128,896]{1,0:T(8,128)(2,1)S(1)}, bf16[128,896]{1,0:T(8,128)(2,1)S(1)}, u32[]{:S(2)}, u32[]{:S(2)}) collective-permute-start(bf16[128,896]{1,0:T(8,128)(2,1)S(1)} %get-tuple-element.81), channel_id=1, source_target_pairs={{0,20},{1,21},{2,22},{3,23},{4,24},{5,25},{6,26},{7,27},{8,28},{9,... | collective-permute-start | bytes 688136 | tf_op jit(solution)/shard_map/ppermute | solution.py:21
  173.0 30.4 %collective-permute-start.29 = (bf16[128,896]{1,0:T(8,128)(2,1)S(1)}, bf16[128,896]{1,0:T(8,128)(2,1)S(1)}, u32[]{:S(2)}, u32[]{:S(2)}) collective-permute-start(bf16[128,896]{1,0:T(8,128)(2,1)S(1)} %get-tuple-element.82), channel_id=1, source_target_pairs={{0,12},{1,13},{2,14},{3,15},{4,16},{5,17},{6,18},{7,19},{8,20},{9,... | collective-permute-start | bytes 688136 | tf_op jit(solution)/shard_map/ppermute | solution.py:21
  (9 other events, 73.3 us)

commit v3 on v2

--- a/solution.py
+++ b/solution.py
@@ -9,7 +9,7 @@
 
 BF16, F32 = jnp.bfloat16, jnp.float32
 NX, CORES = 4, 2
-CHUNKS = ((1, -1, 2, -2), (0, 4, 3, -3))
+CHUNKS = ((3, -3, 2, -2), (0, 4, 1, -1))
 VMEM = pl.BlockSpec(memory_space=pltpu.VMEM)
 SMEM = pl.BlockSpec(memory_space=pltpu.SMEM)
 HBM = pl.BlockSpec(memory_space=pltpu.HBM)
@@ -234,7 +234,7 @@
             moved=1 << 19,
         )(*(pltpu.with_memory_space_constraint(v, pltpu.HBM) for v in (tokens, routes.T, combine.T)))
     }
-    for d in (1, -1, 2, -2):
+    for d in (1, -1, 2, -2, 3, -3):
         step = 1 if d > 0 else -1
         block[d] = along_expert(block[d - step], step, 0)
     chosen = []
@@ -242,10 +242,7 @@
         nz = len(chunk)
         held = nz * capacity
         if chunk == CHUNKS[1]:
-            own, ahead, behind, chosen = lax.optimization_barrier(
-                (block[0], block[2], block[-2], chosen)
-            )
-            block[3], block[-3] = along_expert(ahead, 1, 0), along_expert(behind, -1, 0)
+            own, chosen = lax.optimization_barrier((block[0], chosen))
             block[4] = along_expert(own, 4, 0)
         chosen.append(
             call(
@@ -292,17 +289,19 @@
         )(at, parts, others, down_weight)
 
     def mix(chunk, back, code, weight):
-        mixed = call(
+        return call(
             functools.partial(mix_kernel, held, rows, len(back) == 4),
             [shape(rows, width)] * len(chunk),
             [SMEM] + [VMEM] * (len(back) + 2),
             flops=16 * held * len(chunk) * rows * width,
             moved=2 << 20,
         )(at, *back, code, weight)
-        return [along_expert(m, -d, 0) if d else m for d, m in zip(chunk, mixed)]
-
-    near, far = CHUNKS
-    held = len(near) * capacity
+
+    def add(*values):
+        return sum(v.astype(F32) for v in values).astype(BF16)
+
+    far, near = CHUNKS
+    held = len(far) * capacity
     (first, *first_codes), (second, *second_codes) = chosen
     came = swap_x(first)
     came_second = swap_x(second)
@@ -325,8 +324,15 @@
     others = along_section(parts, 0, 1)
     out_second = contract(parts, others, True)
     back_second = [along_expert(v, 0, d) if d else v for d, v in enumerate(out_second)]
-    partials = mix(near, back, *first_codes) + mix(far, back_second, *second_codes)
-    return sum(p.astype(F32) for p in partials).astype(BF16)
+    up_3, down_3, up_2, down_2 = mix(far, back, *first_codes)
+    own, across, up_1, down_1 = mix(near, back_second, *second_codes)
+    up_2 = add(up_2, along_expert(up_3, -1, 0))
+    down_2 = add(down_2, along_expert(down_3, 1, 0))
+    up_1 = add(up_1, along_expert(up_2, -1, 0))
+    down_1 = add(down_1, along_expert(down_2, 1, 0))
+    return add(
+        own, along_expert(across, -4, 0), along_expert(up_1, -1, 0), along_expert(down_1, 1, 0)
+    )
 
 
 def solution(mesh):

time: 205 us -> 202 us (0.985)
  waiting for transfers between devices: 103 us -> 96.6 us
  starting transfers between devices: 60.7 us -> 63.7 us
    ppermute x17, waiting for transfers between devices: 62 us -> 55.1 us  [along_expert(): lax.ppermute(value, 'expert', [(i, (i // NX + dz) % planes * NX + (i % NX...]
    ppermute x17, starting transfers between devices: 28.2 us -> 30.7 us  [along_expert(): lax.ppermute(value, 'expert', [(i, (i // NX + dz) % planes * NX + (i % NX...]
  transfers between devices with their start and end apart: 33 -> 33, of which waited for: 18 -> 17; matrix products, arithmetic and copies ran while one was open for 0% -> 0% of each run, Pallas kernels for 17% -> 17%
where the time goes in v3:
time: 202 us; the launch traced here: 201 us
  waiting for transfers between devices  96.6 us (48%)
  starting transfers between devices  63.7 us (32%)
  Pallas kernels  38.7 us (19%)
    ppermute x17, waiting for transfers between devices, along_expert(): lax.ppermute(value, 'expert', [(i, (i // NX + dz) % planes * NX + (i % NX...  55.1 us
    ppermute x13, waiting for transfers between devices, along_section(): lax.ppermute(value, 'section', [(i, (i + CORES * dy) % count ^ flip) for...  36.1 us
    ppermute x17, starting transfers between devices, along_expert(): lax.ppermute(value, 'expert', [(i, (i // NX + dz) % planes * NX + (i % NX...  30.7 us
    ppermute x13, starting transfers between devices, along_section(): lax.ppermute(value, 'section', [(i, (i + CORES * dy) % count ^ flip) for...  21 us
    pallas_call x4, Pallas kernels, expand(): call(functools.partial(up_kernel, held, flip), shape(4, 2, held, units),...  16.6 us
    all_to_all x3, starting transfers between devices, swap_x(): lax.all_to_all(value, 'expert', 0, 0, axis_index_groups=x_groups, tiled=T...  12 us
    pallas_call x2, Pallas kernels, contract(): call(functools.partial(down_kernel, held), [shape(2, held, width)] * 4 if...  10.4 us
    pallas_call x2, Pallas kernels, body(): call(functools.partial(select_kernel, capacity, rows), [shape(4, 2 * held...  5.53 us
  transfers between devices with their start and end apart: 33, of which 17 were waited for; matrix products, arithmetic and copies ran while one was open for 0% of the time, Pallas kernels for 17%

profile of v3, /device:TPU:1, one launch (start us, length us, event | category | flops | bytes accessed | tf_op | source)
XLA Modules:
  0.0 200.6 jit_solution(3797504836288932948)
XLA Ops:
  1.0 6.5 %collective-permute-start.3 = (bf16[144,896]{1,0:T(8,128)(2,1)S(1)}, bf16[144,896]{1,0:T(8,128)(2,1)S(1)}, u32[]{:S(2)}, u32[]{:S(2)}) collective-permute-start(bf16[144,896]{1,0:T(8,128)(2,1)S(1)} %shard_map.64.refs_0_), channel_id=1, source_target_pairs={{0,28},{1,29},{2,30},{3,31},{4,0},{5,1},{6,2},{7,3},{8,4},{9,5},{1... | collective-permute-start | bytes 774152 | tf_op jit(solution)/shard_map/ppermute | solution.py:21
  7.5 4.9 %collective-permute-done.3.refs_3_ = bf16[144,896]{1,0:T(8,128)(2,1)S(1)} collective-permute-done((bf16[144,896]{1,0:T(8,128)(2,1)S(1)}, bf16[144,896]{1,0:T(8,128)(2,1)S(1)}, u32[]{:S(2)}, u32[]{:S(2)}) %collective-permute-start.3) | collective-permute-done | bytes 258080 | tf_op jit(solution)/shard_map/ppermute | solution.py:21
  12.4 3.4 %collective-permute-start.4 = (bf16[144,896]{1,0:T(8,128)(2,1)S(1)}, bf16[144,896]{1,0:T(8,128)(2,1)S(1)}, u32[]{:S(2)}, u32[]{:S(2)}) collective-permute-start(bf16[144,896]{1,0:T(8,128)(2,1)S(1)} %collective-permute-done.3.refs_3_), channel_id=1, source_target_pairs={{0,28},{1,29},{2,30},{3,31},{4,0},{5,1},{6,2},{7,3},{8,4},{9,5},{1... | collective-permute-start | bytes 774152 | tf_op jit(solution)/shard_map/ppermute | solution.py:21
  15.8 4.0 %collective-permute-done.4.refs_3_ = bf16[144,896]{1,0:T(8,128)(2,1)S(1)} collective-permute-done((bf16[144,896]{1,0:T(8,128)(2,1)S(1)}, bf16[144,896]{1,0:T(8,128)(2,1)S(1)}, u32[]{:S(2)}, u32[]{:S(2)}) %collective-permute-start.4) | collective-permute-done | bytes 258080 | tf_op jit(solution)/shard_map/ppermute | solution.py:21
  19.7 3.4 %collective-permute-start.5 = (bf16[144,896]{1,0:T(8,128)(2,1)S(1)}, bf16[144,896]{1,0:T(8,128)(2,1)S(1)}, u32[]{:S(2)}, u32[]{:S(2)}) collective-permute-start(bf16[144,896]{1,0:T(8,128)(2,1)S(1)} %collective-permute-done.4.refs_3_), channel_id=1, source_target_pairs={{0,28},{1,29},{2,30},{3,31},{4,0},{5,1},{6,2},{7,3},{8,4},{9,5},{1... | collective-permute-start | bytes 774152 | tf_op jit(solution)/shard_map/ppermute | solution.py:21
  34.0 4.0 %all-to-all-start = ((bf16[4,192,896]{2,1,0:T(8,128)(2,1)}), bf16[4,192,896]{2,1,0:T(8,128)(2,1)S(1)}, u32[]{:S(2)}, u32[]{:S(2)}) async-start(bf16[4,192,896]{2,1,0:T(8,128)(2,1)} %get-tuple-element.45), calls=%async_computation | async-start | bytes 2752512 | tf_op jit(solution)/shard_map/all_to_all | solution.py:217
  38.0 8.7 %collective-permute-done.10.refs_1_ = bf16[144,896]{1,0:T(8,128)(2,1)S(1)} collective-permute-done((bf16[144,896]{1,0:T(8,128)(2,1)S(1)}, bf16[144,896]{1,0:T(8,128)(2,1)S(1)}, u32[]{:S(2)}, u32[]{:S(2)}) %collective-permute-start.10) | collective-permute-done | bytes 258080 | tf_op jit(solution)/shard_map/ppermute | solution.py:21
  52.1 3.5 %all-to-all-start.1 = ((bf16[4,192,896]{2,1,0:T(8,128)(2,1)}), bf16[4,192,896]{2,1,0:T(8,128)(2,1)S(1)}, u32[]{:S(2)}, u32[]{:S(2)}) async-start(bf16[4,192,896]{2,1,0:T(8,128)(2,1)} %get-tuple-element.51), calls=%async_computation.1 | async-start | bytes 2752512 | tf_op jit(solution)/shard_map/all_to_all | solution.py:217
  55.7 4.2 %shard_map.67 = bf16[4,2,96,1024]{3,2,1,0:T(8,128)(2,1)S(1)} custom-call(s32[4]{0:T(128)S(1)} %pad_add_fusion.at_ref, bf16[4,192,896]{2,1,0:T(8,128)(2,1)S(1)} %all-to-all-done.rows_ref, bf16[2,896,1024]{2,1,0:T(8,128)(2,1)} %gate_ref.7, bf16[2,896,1024]{2,1,0:T(8,128)(2,1)} %up_ref.7), custom_call_target="tpu_custom_call" | custom-call | flops 22548578304 | bytes 100663296 | tf_op jit(solution)/shard_map/pallas_call | solution.py:259
  59.8 5.6 %collective-permute-start.6 = (bf16[4,2,96,1024]{3,2,1,0:T(8,128)(2,1)S(1)}, bf16[4,2,96,1024]{3,2,1,0:T(8,128)(2,1)S(1)}, u32[]{:S(2)}, u32[]{:S(2)}) collective-permute-start(bf16[4,2,96,1024]{3,2,1,0:T(8,128)(2,1)S(1)} %shard_map.67), channel_id=1, source_target_pairs={{0,32},{32,0},{64,96},{96,64},{128,160},{160,128},{192,224},{224,1... | collective-permute-start | bytes 4718600 | tf_op jit(solution)/shard_map/ppermute | solution.py:30
  65.4 4.2 %shard_map.66.keep_ref = bf16[4,2,96,1024]{3,2,1,0:T(8,128)(2,1)S(1)} custom-call(s32[4]{0:T(128)S(1)} %pad_add_fusion.at_ref, bf16[4,192,896]{2,1,0:T(8,128)(2,1)S(1)} %all-to-all-done.rows_ref, bf16[2,896,1024]{2,1,0:T(8,128)(2,1)} %gate_ref.7, bf16[2,896,1024]{2,1,0:T(8,128)(2,1)} %up_ref.7), custom_call_target="tpu_custom_call" | custom-call | flops 22548578304 | bytes 100663296 | tf_op jit(solution)/shard_map/pallas_call | solution.py:259
  75.8 4.2 %shard_map.71 = bf16[4,2,96,1024]{3,2,1,0:T(8,128)(2,1)S(1)} custom-call(s32[4]{0:T(128)S(1)} %pad_add_fusion.at_ref, bf16[4,192,896]{2,1,0:T(8,128)(2,1)S(1)} %all-to-all-done.1.rows_ref, bf16[2,896,1024]{2,1,0:T(8,128)(2,1)} %gate_ref.7, bf16[2,896,1024]{2,1,0:T(8,128)(2,1)} %up_ref.7), custom_call_target="tpu_custom_call" | custom-call | flops 22548578304 | bytes 100663296 | tf_op jit(solution)/shard_map/pallas_call | solution.py:259
  80.9 4.2 %shard_map.70.refs_4_ = bf16[4,2,96,1024]{3,2,1,0:T(8,128)(2,1)S(1)} custom-call(s32[4]{0:T(128)S(1)} %pad_add_fusion.at_ref, bf16[4,192,896]{2,1,0:T(8,128)(2,1)S(1)} %all-to-all-done.1.rows_ref, bf16[2,896,1024]{2,1,0:T(8,128)(2,1)} %gate_ref.7, bf16[2,896,1024]{2,1,0:T(8,128)(2,1)} %up_ref.7), custom_call_target="tpu_custom_call" | custom-call | flops 22548578304 | bytes 100663296 | tf_op jit(solution)/shard_map/pallas_call | solution.py:259
  85.0 7.6 %collective-permute-done.8.refs_2_ = bf16[2,96,1024]{2,1,0:T(8,128)(2,1)S(1)} collective-permute-done((bf16[2,96,1024]{2,1,0:T(8,128)(2,1)}, bf16[2,96,1024]{2,1,0:T(8,128)(2,1)S(1)}, u32[]{:S(2)}, u32[]{:S(2)}) %collective-permute-start.8) | collective-permute-done | bytes 393248 | tf_op jit(solution)/shard_map/ppermute | solution.py:30
  97.3 11.2 %collective-permute-done.12.refs_1_ = bf16[3,96,1024]{2,1,0:T(8,128)(2,1)S(1)} collective-permute-done((bf16[3,96,1024]{2,1,0:T(8,128)(2,1)S(1)}, bf16[3,96,1024]{2,1,0:T(8,128)(2,1)S(1)}, u32[]{:S(2)}, u32[]{:S(2)}) %collective-permute-start.12) | collective-permute-done | bytes 589856 | tf_op jit(solution)/shard_map/ppermute | solution.py:30
  108.6 13.6 %collective-permute-done.13.refs_2_ = bf16[3,96,1024]{2,1,0:T(8,128)(2,1)S(1)} collective-permute-done((bf16[3,96,1024]{2,1,0:T(8,128)(2,1)S(1)}, bf16[3,96,1024]{2,1,0:T(8,128)(2,1)S(1)}, u32[]{:S(2)}, u32[]{:S(2)}) %collective-permute-start.13) | collective-permute-done | bytes 589856 | tf_op jit(solution)/shard_map/ppermute | solution.py:30
  127.2 5.4 %shard_map.74 = bf16[4,2,96,896]{3,2,1,0:T(8,128)(2,1)} custom-call(s32[4]{0:T(128)S(1)} %pad_add_fusion.at_ref, bf16[4,96,1024]{2,1,0:T(8,128)(2,1)S(1)} %pad_maximum_fusion.own_ref, bf16[4,96,1024]{2,1,0:T(8,128)(2,1)S(1)} %collective-permute-done.18.other_ref, bf16[2,1024,896]{2,1,0:T(8,128)(2,1)} %down_ref.3), custom_call_target="tpu_custom_call" | custom-call | bytes 16384 | tf_op jit(solution)/shard_map/pallas_call | solution.py:279
  132.5 4.5 %all-to-all-start.2 = ((bf16[4,2,96,896]{3,2,1,0:T(8,128)(2,1)}), bf16[4,2,96,896]{3,2,1,0:T(8,128)(2,1)S(1)}, u32[]{:S(2)}, u32[]{:S(2)}) async-start(bf16[4,2,96,896]{3,2,1,0:T(8,128)(2,1)} %shard_map.74), calls=%async_computation.2 | async-start | bytes 2752512 | tf_op jit(solution)/shard_map/all_to_all | solution.py:217
  141.7 5.0 %shard_map.75 = (bf16[2,96,896]{2,1,0:T(8,128)(2,1)S(1)}, bf16[2,96,896]{2,1,0:T(8,128)(2,1)}, bf16[2,96,896]{2,1,0:T(8,128)(2,1)}, bf16[2,96,896]{2,1,0:T(8,128)(2,1)S(1)}) custom-call(s32[4]{0:T(128)S(1)} %pad_add_fusion.at_ref, bf16[4,96,1024]{2,1,0:T(8,128)(2,1)S(1)} %pad_maximum_fusion.1.own_ref, ...), custom_call_target="tpu_custom_call" | custom-call | bytes 16384 | tf_op jit(solution)/shard_map/pallas_call | solution.py:279
  158.0 6.8 %collective-permute-done.20.refs_1_ = bf16[2,96,896]{2,1,0:T(8,128)(2,1)S(1)} collective-permute-done((bf16[2,96,896]{2,1,0:T(8,128)(2,1)}, bf16[2,96,896]{2,1,0:T(8,128)(2,1)S(1)}, u32[]{:S(2)}, u32[]{:S(2)}) %collective-permute-start.20) | collective-permute-done | bytes 344096 | tf_op jit(solution)/shard_map/ppermute | solution.py:21
  164.8 4.8 %collective-permute-done.21.refs_2_ = bf16[2,96,896]{2,1,0:T(8,128)(2,1)S(1)} collective-permute-done((bf16[2,96,896]{2,1,0:T(8,128)(2,1)}, bf16[2,96,896]{2,1,0:T(8,128)(2,1)S(1)}, u32[]{:S(2)}, u32[]{:S(2)}) %collective-permute-start.21) | collective-permute-done | bytes 344096 | tf_op jit(solution)/shard_map/ppermute | solution.py:21
  171.2 3.7 %collective-permute-start.23 = (bf16[128,896]{1,0:T(8,128)(2,1)S(1)}, bf16[128,896]{1,0:T(8,128)(2,1)S(1)}, u32[]{:S(2)}, u32[]{:S(2)}) collective-permute-start(bf16[128,896]{1,0:T(8,128)(2,1)S(1)} %get-tuple-element.70), channel_id=1, source_target_pairs={{0,16},{1,17},{2,18},{3,19},{4,20},{5,21},{6,22},{7,23},{8,24},{9,... | collective-permute-start | bytes 688136 | tf_op jit(solution)/shard_map/ppermute | solution.py:21
  176.6 12.1 %collective-permute-done.25 = bf16[128,896]{1,0:T(8,128)(2,1)S(1)} collective-permute-done((bf16[128,896]{1,0:T(8,128)(2,1)S(1)}, bf16[128,896]{1,0:T(8,128)(2,1)S(1)}, u32[]{:S(2)}, u32[]{:S(2)}) %collective-permute-start.25) | collective-permute-done | bytes 229408 | tf_op jit(solution)/shard_map/ppermute | solution.py:21
  192.3 4.3 %collective-permute-done.26 = bf16[128,896]{1,0:T(8,128)(2,1)S(1)} collective-permute-done((bf16[128,896]{1,0:T(8,128)(2,1)S(1)}, bf16[128,896]{1,0:T(8,128)(2,1)S(1)}, u32[]{:S(2)}, u32[]{:S(2)}) %collective-permute-start.26) | collective-permute-done | bytes 229408 | tf_op jit(solution)/shard_map/ppermute | solution.py:21
  (68 shorter events, 60.8 us)
Async XLA Ops:
  1.0 11.4 %collective-permute-start.3 = (bf16[144,896]{1,0:T(8,128)(2,1)S(1)}, bf16[144,896]{1,0:T(8,128)(2,1)S(1)}, u32[]{:S(2)}, u32[]{:S(2)}) collective-permute-start(bf16[144,896]{1,0:T(8,128)(2,1)S(1)} %shard_map.64.refs_0_), channel_id=1, source_target_pairs={{0,28},{1,29},{2,30},{3,31},{4,0},{5,1},{6,2},{7,3},{8,4},{9,5},{1... | collective-permute-start | bytes 774152 | tf_op jit(solution)/shard_map/ppermute | solution.py:21
  32.3 14.4 %collective-permute-start.10 = (bf16[144,896]{1,0:T(8,128)(2,1)S(1)}, bf16[144,896]{1,0:T(8,128)(2,1)S(1)}, u32[]{:S(2)}, u32[]{:S(2)}) collective-permute-start(bf16[144,896]{1,0:T(8,128)(2,1)S(1)} %shard_map.64.refs_0_), channel_id=1, source_target_pairs={{0,16},{1,17},{2,18},{3,19},{4,20},{5,21},{6,22},{7,23},{8,24},{9,... | collective-permute-start | bytes 774152 | tf_op jit(solution)/shard_map/ppermute | solution.py:21
  34.0 18.1 %all-to-all-start = ((bf16[4,192,896]{2,1,0:T(8,128)(2,1)}), bf16[4,192,896]{2,1,0:T(8,128)(2,1)S(1)}, u32[]{:S(2)}, u32[]{:S(2)}) async-start(bf16[4,192,896]{2,1,0:T(8,128)(2,1)} %get-tuple-element.45), calls=%async_computation | async-start | bytes 2752512 | tf_op jit(solution)/shard_map/all_to_all | solution.py:217
  52.1 23.6 %all-to-all-start.1 = ((bf16[4,192,896]{2,1,0:T(8,128)(2,1)}), bf16[4,192,896]{2,1,0:T(8,128)(2,1)S(1)}, u32[]{:S(2)}, u32[]{:S(2)}) async-start(bf16[4,192,896]{2,1,0:T(8,128)(2,1)} %get-tuple-element.51), calls=%async_computation.1 | async-start | bytes 2752512 | tf_op jit(solution)/shard_map/all_to_all | solution.py:217
  59.8 9.7 %collective-permute-start.6 = (bf16[4,2,96,1024]{3,2,1,0:T(8,128)(2,1)S(1)}, bf16[4,2,96,1024]{3,2,1,0:T(8,128)(2,1)S(1)}, u32[]{:S(2)}, u32[]{:S(2)}) collective-permute-start(bf16[4,2,96,1024]{3,2,1,0:T(8,128)(2,1)S(1)} %shard_map.67), channel_id=1, source_target_pairs={{0,32},{32,0},{64,96},{96,64},{128,160},{160,128},{192,224},{224,1... | collective-permute-start | bytes 4718600 | tf_op jit(solution)/shard_map/ppermute | solution.py:30
  70.8 14.3 %collective-permute-start.7 = (bf16[2,96,1024]{2,1,0:T(8,128)(2,1)}, bf16[2,96,1024]{2,1,0:T(8,128)(2,1)S(1)}, u32[]{:S(2)}, u32[]{:S(2)}) collective-permute-start(bf16[2,96,1024]{2,1,0:T(8,128)(2,1)} %get-tuple-element.47), channel_id=1, source_target_pairs={{0,64},{32,96},{64,128},{96,160},{128,192},{160,224},{192,0},{224,... | collective-permute-start | bytes 1179656 | tf_op jit(solution)/shard_map/ppermute | solution.py:30
  72.1 20.5 %collective-permute-start.8 = (bf16[2,96,1024]{2,1,0:T(8,128)(2,1)}, bf16[2,96,1024]{2,1,0:T(8,128)(2,1)S(1)}, u32[]{:S(2)}, u32[]{:S(2)}) collective-permute-start(bf16[2,96,1024]{2,1,0:T(8,128)(2,1)} %get-tuple-element.48), channel_id=1, source_target_pairs={{0,128},{32,160},{64,192},{96,224},{128,0},{160,32},{192,64},{224,... | collective-permute-start | bytes 1179656 | tf_op jit(solution)/shard_map/ppermute | solution.py:30
  74.7 17.9 %collective-permute-start.9 = (bf16[2,96,1024]{2,1,0:T(8,128)(2,1)S(1)}, bf16[2,96,1024]{2,1,0:T(8,128)(2,1)S(1)}, u32[]{:S(2)}, u32[]{:S(2)}) collective-permute-start(bf16[2,96,1024]{2,1,0:T(8,128)(2,1)S(1)} %get-tuple-element.49), channel_id=1, source_target_pairs={{0,192},{32,224},{64,0},{96,32},{128,64},{160,96},{192,128},{224,1... | collective-permute-start | bytes 1179656 | tf_op jit(solution)/shard_map/ppermute | solution.py:30
  79.9 12.7 %collective-permute-start.11 = (bf16[4,2,96,1024]{3,2,1,0:T(8,128)(2,1)S(1)}, bf16[4,2,96,1024]{3,2,1,0:T(8,128)(2,1)S(1)}, u32[]{:S(2)}, u32[]{:S(2)}) collective-permute-start(bf16[4,2,96,1024]{3,2,1,0:T(8,128)(2,1)S(1)} %shard_map.71), channel_id=1, source_target_pairs={{0,32},{32,0},{64,96},{96,64},{128,160},{160,128},{192,224},{224,1... | collective-permute-start | bytes 4718600 | tf_op jit(solution)/shard_map/ppermute | solution.py:30
  93.2 15.3 %collective-permute-start.12 = (bf16[3,96,1024]{2,1,0:T(8,128)(2,1)S(1)}, bf16[3,96,1024]{2,1,0:T(8,128)(2,1)S(1)}, u32[]{:S(2)}, u32[]{:S(2)}) collective-permute-start(bf16[3,96,1024]{2,1,0:T(8,128)(2,1)S(1)} %get-tuple-element.54), channel_id=1, source_target_pairs={{0,64},{32,96},{64,128},{96,160},{128,192},{160,224},{192,0},{224,... | collective-permute-start | bytes 1769480 | tf_op jit(solution)/shard_map/ppermute | solution.py:30
  93.4 28.8 %collective-permute-start.13 = (bf16[3,96,1024]{2,1,0:T(8,128)(2,1)S(1)}, bf16[3,96,1024]{2,1,0:T(8,128)(2,1)S(1)}, u32[]{:S(2)}, u32[]{:S(2)}) collective-permute-start(bf16[3,96,1024]{2,1,0:T(8,128)(2,1)S(1)} %get-tuple-element.55), channel_id=1, source_target_pairs={{0,128},{32,160},{64,192},{96,224},{128,0},{160,32},{192,64},{224,... | collective-permute-start | bytes 1769480 | tf_op jit(solution)/shard_map/ppermute | solution.py:30
  96.6 25.6 %collective-permute-start.14 = (bf16[3,96,1024]{2,1,0:T(8,128)(2,1)S(1)}, bf16[3,96,1024]{2,1,0:T(8,128)(2,1)S(1)}, u32[]{:S(2)}, u32[]{:S(2)}) collective-permute-start(bf16[3,96,1024]{2,1,0:T(8,128)(2,1)S(1)} %get-tuple-element.56), channel_id=1, source_target_pairs={{0,192},{32,224},{64,0},{96,32},{128,64},{160,96},{192,128},{224,1... | collective-permute-start | bytes 1769480 | tf_op jit(solution)/shard_map/ppermute | solution.py:30
  124.0 13.1 %collective-permute-start.17 = (bf16[96,1024]{1,0:T(8,128)(2,1)S(1)}, bf16[96,1024]{1,0:T(8,128)(2,1)S(1)}, u32[]{:S(2)}, u32[]{:S(2)}) collective-permute-start(bf16[96,1024]{1,0:T(8,128)(2,1)S(1)} %shard_map.73), channel_id=1, source_target_pairs={{0,192},{32,224},{64,0},{96,32},{128,64},{160,96},{192,128},{224,1... | collective-permute-start | bytes 589832 | tf_op jit(solution)/shard_map/ppermute | solution.py:30
  126.4 10.6 %collective-permute-start.16 = (bf16[96,1024]{1,0:T(8,128)(2,1)S(1)}, bf16[96,1024]{1,0:T(8,128)(2,1)S(1)}, u32[]{:S(2)}, u32[]{:S(2)}) collective-permute-start(bf16[96,1024]{1,0:T(8,128)(2,1)S(1)} %shard_map.73), channel_id=1, source_target_pairs={{0,128},{32,160},{64,192},{96,224},{128,0},{160,32},{192,64},{224,... | collective-permute-start | bytes 589832 | tf_op jit(solution)/shard_map/ppermute | solution.py:30
  127.1 11.8 %collective-permute-start.15 = (bf16[96,1024]{1,0:T(8,128)(2,1)S(1)}, bf16[96,1024]{1,0:T(8,128)(2,1)S(1)}, u32[]{:S(2)}, u32[]{:S(2)}) collective-permute-start(bf16[96,1024]{1,0:T(8,128)(2,1)S(1)} %shard_map.73), channel_id=1, source_target_pairs={{0,64},{32,96},{64,128},{96,160},{128,192},{160,224},{192,0},{224,... | collective-permute-start | bytes 589832 | tf_op jit(solution)/shard_map/ppermute | solution.py:30
  132.5 22.3 %all-to-all-start.2 = ((bf16[4,2,96,896]{3,2,1,0:T(8,128)(2,1)}), bf16[4,2,96,896]{3,2,1,0:T(8,128)(2,1)S(1)}, u32[]{:S(2)}, u32[]{:S(2)}) async-start(bf16[4,2,96,896]{3,2,1,0:T(8,128)(2,1)} %shard_map.74), calls=%async_computation.2 | async-start | bytes 2752512 | tf_op jit(solution)/shard_map/all_to_all | solution.py:217
  146.8 18.0 %collective-permute-start.20 = (bf16[2,96,896]{2,1,0:T(8,128)(2,1)}, bf16[2,96,896]{2,1,0:T(8,128)(2,1)S(1)}, u32[]{:S(2)}, u32[]{:S(2)}) collective-permute-start(bf16[2,96,896]{2,1,0:T(8,128)(2,1)} %get-tuple-element.64), channel_id=1, source_target_pairs={{0,1},{1,2},{2,3},{3,0},{4,5},{5,6},{6,7},{7,4},{8,9},{9,10},{10,1... | collective-permute-start | bytes 1032200 | tf_op jit(solution)/shard_map/ppermute | solution.py:21
  148.6 21.0 %collective-permute-start.21 = (bf16[2,96,896]{2,1,0:T(8,128)(2,1)}, bf16[2,96,896]{2,1,0:T(8,128)(2,1)S(1)}, u32[]{:S(2)}, u32[]{:S(2)}) collective-permute-start(bf16[2,96,896]{2,1,0:T(8,128)(2,1)} %get-tuple-element.65), channel_id=1, source_target_pairs={{0,2},{1,3},{2,0},{3,1},{4,6},{5,7},{6,4},{7,5},{8,10},{9,11},{10,... | collective-permute-start | bytes 1032200 | tf_op jit(solution)/shard_map/ppermute | solution.py:21
  151.0 18.6 %collective-permute-start.22 = (bf16[2,96,896]{2,1,0:T(8,128)(2,1)S(1)}, bf16[2,96,896]{2,1,0:T(8,128)(2,1)S(1)}, u32[]{:S(2)}, u32[]{:S(2)}) collective-permute-start(bf16[2,96,896]{2,1,0:T(8,128)(2,1)S(1)} %get-tuple-element.66), channel_id=1, source_target_pairs={{0,3},{1,0},{2,1},{3,2},{4,7},{5,4},{6,5},{7,6},{8,11},{9,8},{10,9... | collective-permute-start | bytes 1032200 | tf_op jit(solution)/shard_map/ppermute | solution.py:21
  156.4 18.5 %collective-permute-start.24 = (bf16[128,896]{1,0:T(8,128)(2,1)S(1)}, bf16[128,896]{1,0:T(8,128)(2,1)S(1)}, u32[]{:S(2)}, u32[]{:S(2)}) collective-permute-start(bf16[128,896]{1,0:T(8,128)(2,1)S(1)} %get-tuple-element.75), channel_id=1, source_target_pairs={{0,28},{1,29},{2,30},{3,31},{4,0},{5,1},{6,2},{7,3},{8,4},{9,5},{1... | collective-permute-start | bytes 688136 | tf_op jit(solution)/shard_map/ppermute | solution.py:21
  156.5 18.5 %collective-permute-start.27 = (bf16[128,896]{1,0:T(8,128)(2,1)S(1)}, bf16[128,896]{1,0:T(8,128)(2,1)S(1)}, u32[]{:S(2)}, u32[]{:S(2)}) collective-permute-start(bf16[128,896]{1,0:T(8,128)(2,1)S(1)} %get-tuple-element.78), channel_id=1, source_target_pairs={{0,4},{1,5},{2,6},{3,7},{4,8},{5,9},{6,10},{7,11},{8,12},{9,13},{1... | collective-permute-start | bytes 688136 | tf_op jit(solution)/shard_map/ppermute | solution.py:21
  171.2 21.1 %collective-permute-start.23 = (bf16[128,896]{1,0:T(8,128)(2,1)S(1)}, bf16[128,896]{1,0:T(8,128)(2,1)S(1)}, u32[]{:S(2)}, u32[]{:S(2)}) collective-permute-start(bf16[128,896]{1,0:T(8,128)(2,1)S(1)} %get-tuple-element.70), channel_id=1, source_target_pairs={{0,16},{1,17},{2,18},{3,19},{4,20},{5,21},{6,22},{7,23},{8,24},{9,... | collective-permute-start | bytes 688136 | tf_op jit(solution)/shard_map/ppermute | solution.py:21
  175.0 13.8 %collective-permute-start.25 = (bf16[128,896]{1,0:T(8,128)(2,1)S(1)}, bf16[128,896]{1,0:T(8,128)(2,1)S(1)}, u32[]{:S(2)}, u32[]{:S(2)}) collective-permute-start(bf16[128,896]{1,0:T(8,128)(2,1)S(1)} %add_convert_fusion.4), channel_id=1, source_target_pairs={{0,28},{1,29},{2,30},{3,31},{4,0},{5,1},{6,2},{7,3},{8,4},{9,5},{1... | collective-permute-start | bytes 688136 | tf_op jit(solution)/shard_map/ppermute | solution.py:21
  175.1 17.0 %collective-permute-start.28 = (bf16[128,896]{1,0:T(8,128)(2,1)S(1)}, bf16[128,896]{1,0:T(8,128)(2,1)S(1)}, u32[]{:S(2)}, u32[]{:S(2)}) collective-permute-start(bf16[128,896]{1,0:T(8,128)(2,1)S(1)} %add_convert_fusion.2), channel_id=1, source_target_pairs={{0,4},{1,5},{2,6},{3,7},{4,8},{5,9},{6,10},{7,11},{8,12},{9,13},{1... | collective-permute-start | bytes 688136 | tf_op jit(solution)/shard_map/ppermute | solution.py:21
  (9 other events, 59.1 us)

commit v4 on v3

--- a/solution.py
+++ b/solution.py
@@ -325,9 +325,10 @@
     out_second = contract(parts, others, True)
     back_second = [along_expert(v, 0, d) if d else v for d, v in enumerate(out_second)]
     up_3, down_3, up_2, down_2 = mix(far, back, *first_codes)
-    own, across, up_1, down_1 = mix(near, back_second, *second_codes)
     up_2 = add(up_2, along_expert(up_3, -1, 0))
     down_2 = add(down_2, along_expert(down_3, 1, 0))
+    back_second, _ = lax.optimization_barrier((back_second, (up_2, down_2)))
+    own, across, up_1, down_1 = mix(near, back_second, *second_codes)
     up_1 = add(up_1, along_expert(up_2, -1, 0))
     down_1 = add(down_1, along_expert(down_2, 1, 0))
     return add(

time: 202 us -> 200 us (0.990)
  starting transfers between devices: 63.7 us -> 59.4 us
  waiting for transfers between devices: 96.6 us -> 99.7 us
    ppermute x13, waiting for transfers between devices: 36.1 us -> 45.8 us  [along_section(): lax.ppermute(value, 'section', [(i, (i + CORES * dy) % count ^ flip) for...]
    ppermute x17, waiting for transfers between devices: 55.1 us -> 48.8 us  [along_expert(): lax.ppermute(value, 'expert', [(i, (i // NX + dz) % planes * NX + (i % NX...]
    ppermute x17, starting transfers between devices: 30.7 us -> 26.6 us  [along_expert(): lax.ppermute(value, 'expert', [(i, (i // NX + dz) % planes * NX + (i % NX...]
  transfers between devices with their start and end apart: 33 -> 33, of which waited for: 17 -> 20; matrix products, arithmetic and copies ran while one was open for 0% -> 0% of each run, Pallas kernels for 17% -> 14%
where the time goes in v4:
time: 200 us; the launch traced here: 199 us
  waiting for transfers between devices  99.7 us (50%)
  starting transfers between devices  59.4 us (30%)
  Pallas kernels  37.9 us (19%)
    ppermute x17, waiting for transfers between devices, along_expert(): lax.ppermute(value, 'expert', [(i, (i // NX + dz) % planes * NX + (i % NX...  48.8 us
    ppermute x13, waiting for transfers between devices, along_section(): lax.ppermute(value, 'section', [(i, (i + CORES * dy) % count ^ flip) for...  45.8 us
    ppermute x17, starting transfers between devices, along_expert(): lax.ppermute(value, 'expert', [(i, (i // NX + dz) % planes * NX + (i % NX...  26.6 us
    ppermute x13, starting transfers between devices, along_section(): lax.ppermute(value, 'section', [(i, (i + CORES * dy) % count ^ flip) for...  20.7 us
    pallas_call x4, Pallas kernels, expand(): call(functools.partial(up_kernel, held, flip), shape(4, 2, held, units),...  16.6 us
    all_to_all x3, starting transfers between devices, swap_x(): lax.all_to_all(value, 'expert', 0, 0, axis_index_groups=x_groups, tiled=T...  12 us
    pallas_call x2, Pallas kernels, contract(): call(functools.partial(down_kernel, held), [shape(2, held, width)] * 4 if...  9.61 us
    pallas_call x2, Pallas kernels, body(): call(functools.partial(select_kernel, capacity, rows), [shape(4, 2 * held...  5.53 us
  transfers between devices with their start and end apart: 33, of which 20 were waited for; matrix products, arithmetic and copies ran while one was open for 0% of the time, Pallas kernels for 14%

profile of v4, /device:TPU:1, one launch (start us, length us, event | category | flops | bytes accessed | tf_op | source)
XLA Modules:
  0.0 198.5 jit_solution(15795804955770299458)
XLA Ops:
  1.0 6.5 %collective-permute-start.3 = (bf16[144,896]{1,0:T(8,128)(2,1)S(1)}, bf16[144,896]{1,0:T(8,128)(2,1)S(1)}, u32[]{:S(2)}, u32[]{:S(2)}) collective-permute-start(bf16[144,896]{1,0:T(8,128)(2,1)S(1)} %shard_map.64.refs_0_), channel_id=1, source_target_pairs={{0,28},{1,29},{2,30},{3,31},{4,0},{5,1},{6,2},{7,3},{8,4},{9,5},{1... | collective-permute-start | bytes 774152 | tf_op jit(solution)/shard_map/ppermute | solution.py:21
  7.5 4.9 %collective-permute-done.3.refs_3_ = bf16[144,896]{1,0:T(8,128)(2,1)S(1)} collective-permute-done((bf16[144,896]{1,0:T(8,128)(2,1)S(1)}, bf16[144,896]{1,0:T(8,128)(2,1)S(1)}, u32[]{:S(2)}, u32[]{:S(2)}) %collective-permute-start.3) | collective-permute-done | bytes 258080 | tf_op jit(solution)/shard_map/ppermute | solution.py:21
  15.8 4.0 %collective-permute-done.4.refs_3_ = bf16[144,896]{1,0:T(8,128)(2,1)S(1)} collective-permute-done((bf16[144,896]{1,0:T(8,128)(2,1)S(1)}, bf16[144,896]{1,0:T(8,128)(2,1)S(1)}, u32[]{:S(2)}, u32[]{:S(2)}) %collective-permute-start.4) | collective-permute-done | bytes 258080 | tf_op jit(solution)/shard_map/ppermute | solution.py:21
  34.0 4.0 %all-to-all-start = ((bf16[4,192,896]{2,1,0:T(8,128)(2,1)}), bf16[4,192,896]{2,1,0:T(8,128)(2,1)S(1)}, u32[]{:S(2)}, u32[]{:S(2)}) async-start(bf16[4,192,896]{2,1,0:T(8,128)(2,1)} %get-tuple-element.49), calls=%async_computation | async-start | bytes 2752512 | tf_op jit(solution)/shard_map/all_to_all | solution.py:217
  38.0 8.7 %collective-permute-done.10.refs_1_ = bf16[144,896]{1,0:T(8,128)(2,1)S(1)} collective-permute-done((bf16[144,896]{1,0:T(8,128)(2,1)S(1)}, bf16[144,896]{1,0:T(8,128)(2,1)S(1)}, u32[]{:S(2)}, u32[]{:S(2)}) %collective-permute-start.10) | collective-permute-done | bytes 258080 | tf_op jit(solution)/shard_map/ppermute | solution.py:21
  52.1 3.5 %all-to-all-start.1 = ((bf16[4,192,896]{2,1,0:T(8,128)(2,1)}), bf16[4,192,896]{2,1,0:T(8,128)(2,1)S(1)}, u32[]{:S(2)}, u32[]{:S(2)}) async-start(bf16[4,192,896]{2,1,0:T(8,128)(2,1)} %get-tuple-element.55), calls=%async_computation.1 | async-start | bytes 2752512 | tf_op jit(solution)/shard_map/all_to_all | solution.py:217
  55.7 4.2 %shard_map.67 = bf16[4,2,96,1024]{3,2,1,0:T(8,128)(2,1)S(1)} custom-call(s32[4]{0:T(128)S(1)} %pad_add_fusion.at_ref, bf16[4,192,896]{2,1,0:T(8,128)(2,1)S(1)} %all-to-all-done.rows_ref, bf16[2,896,1024]{2,1,0:T(8,128)(2,1)} %gate_ref.7, bf16[2,896,1024]{2,1,0:T(8,128)(2,1)} %up_ref.7), custom_call_target="tpu_custom_call" | custom-call | flops 22548578304 | bytes 100663296 | tf_op jit(solution)/shard_map/pallas_call | solution.py:259
  59.8 5.6 %collective-permute-start.6 = (bf16[4,2,96,1024]{3,2,1,0:T(8,128)(2,1)S(1)}, bf16[4,2,96,1024]{3,2,1,0:T(8,128)(2,1)S(1)}, u32[]{:S(2)}, u32[]{:S(2)}) collective-permute-start(bf16[4,2,96,1024]{3,2,1,0:T(8,128)(2,1)S(1)} %shard_map.67), channel_id=1, source_target_pairs={{0,32},{32,0},{64,96},{96,64},{128,160},{160,128},{192,224},{224,1... | collective-permute-start | bytes 4718600 | tf_op jit(solution)/shard_map/ppermute | solution.py:30
  65.4 4.2 %shard_map.66.keep_ref = bf16[4,2,96,1024]{3,2,1,0:T(8,128)(2,1)S(1)} custom-call(s32[4]{0:T(128)S(1)} %pad_add_fusion.at_ref, bf16[4,192,896]{2,1,0:T(8,128)(2,1)S(1)} %all-to-all-done.rows_ref, bf16[2,896,1024]{2,1,0:T(8,128)(2,1)} %gate_ref.7, bf16[2,896,1024]{2,1,0:T(8,128)(2,1)} %up_ref.7), custom_call_target="tpu_custom_call" | custom-call | flops 22548578304 | bytes 100663296 | tf_op jit(solution)/shard_map/pallas_call | solution.py:259
  75.8 4.2 %shard_map.71 = bf16[4,2,96,1024]{3,2,1,0:T(8,128)(2,1)S(1)} custom-call(s32[4]{0:T(128)S(1)} %pad_add_fusion.at_ref, bf16[4,192,896]{2,1,0:T(8,128)(2,1)S(1)} %all-to-all-done.1.rows_ref, bf16[2,896,1024]{2,1,0:T(8,128)(2,1)} %gate_ref.7, bf16[2,896,1024]{2,1,0:T(8,128)(2,1)} %up_ref.7), custom_call_target="tpu_custom_call" | custom-call | flops 22548578304 | bytes 100663296 | tf_op jit(solution)/shard_map/pallas_call | solution.py:259
  80.9 4.2 %shard_map.70.refs_4_ = bf16[4,2,96,1024]{3,2,1,0:T(8,128)(2,1)S(1)} custom-call(s32[4]{0:T(128)S(1)} %pad_add_fusion.at_ref, bf16[4,192,896]{2,1,0:T(8,128)(2,1)S(1)} %all-to-all-done.1.rows_ref, bf16[2,896,1024]{2,1,0:T(8,128)(2,1)} %gate_ref.7, bf16[2,896,1024]{2,1,0:T(8,128)(2,1)} %up_ref.7), custom_call_target="tpu_custom_call" | custom-call | flops 22548578304 | bytes 100663296 | tf_op jit(solution)/shard_map/pallas_call | solution.py:259
  85.0 7.6 %collective-permute-done.8.refs_2_ = bf16[2,96,1024]{2,1,0:T(8,128)(2,1)S(1)} collective-permute-done((bf16[2,96,1024]{2,1,0:T(8,128)(2,1)}, bf16[2,96,1024]{2,1,0:T(8,128)(2,1)S(1)}, u32[]{:S(2)}, u32[]{:S(2)}) %collective-permute-start.8) | collective-permute-done | bytes 393248 | tf_op jit(solution)/shard_map/ppermute | solution.py:30
  97.3 11.2 %collective-permute-done.12.refs_1_ = bf16[3,96,1024]{2,1,0:T(8,128)(2,1)S(1)} collective-permute-done((bf16[3,96,1024]{2,1,0:T(8,128)(2,1)S(1)}, bf16[3,96,1024]{2,1,0:T(8,128)(2,1)S(1)}, u32[]{:S(2)}, u32[]{:S(2)}) %collective-permute-start.12) | collective-permute-done | bytes 589856 | tf_op jit(solution)/shard_map/ppermute | solution.py:30
  108.6 13.6 %collective-permute-done.13.refs_2_ = bf16[3,96,1024]{2,1,0:T(8,128)(2,1)S(1)} collective-permute-done((bf16[3,96,1024]{2,1,0:T(8,128)(2,1)S(1)}, bf16[3,96,1024]{2,1,0:T(8,128)(2,1)S(1)}, u32[]{:S(2)}, u32[]{:S(2)}) %collective-permute-start.13) | collective-permute-done | bytes 589856 | tf_op jit(solution)/shard_map/ppermute | solution.py:30
  125.6 5.4 %shard_map.74 = bf16[4,2,96,896]{3,2,1,0:T(8,128)(2,1)} custom-call(s32[4]{0:T(128)S(1)} %pad_add_fusion.at_ref, bf16[4,96,1024]{2,1,0:T(8,128)(2,1)S(1)} %pad_maximum_fusion.own_ref, bf16[4,96,1024]{2,1,0:T(8,128)(2,1)S(1)} %collective-permute-done.18.other_ref, bf16[2,1024,896]{2,1,0:T(8,128)(2,1)} %down_ref.3), custom_call_target="tpu_custom_call" | custom-call | bytes 16384 | tf_op jit(solution)/shard_map/pallas_call | solution.py:279
  131.0 4.5 %all-to-all-start.2 = ((bf16[4,2,96,896]{3,2,1,0:T(8,128)(2,1)}), bf16[4,2,96,896]{3,2,1,0:T(8,128)(2,1)S(1)}, u32[]{:S(2)}, u32[]{:S(2)}) async-start(bf16[4,2,96,896]{3,2,1,0:T(8,128)(2,1)} %shard_map.74), calls=%async_computation.2 | async-start | bytes 2752512 | tf_op jit(solution)/shard_map/all_to_all | solution.py:217
  138.6 3.5 %collective-permute-done.17 = bf16[96,1024]{1,0:T(8,128)(2,1)S(1)} collective-permute-done((bf16[96,1024]{1,0:T(8,128)(2,1)S(1)}, bf16[96,1024]{1,0:T(8,128)(2,1)S(1)}, u32[]{:S(2)}, u32[]{:S(2)}) %collective-permute-start.17) | collective-permute-done | bytes 196640 | tf_op jit(solution)/shard_map/ppermute | solution.py:30
  144.9 5.5 %collective-permute-done.15 = bf16[96,1024]{1,0:T(8,128)(2,1)S(1)} collective-permute-done((bf16[96,1024]{1,0:T(8,128)(2,1)S(1)}, bf16[96,1024]{1,0:T(8,128)(2,1)S(1)}, u32[]{:S(2)}, u32[]{:S(2)}) %collective-permute-start.15) | collective-permute-done | bytes 196640 | tf_op jit(solution)/shard_map/ppermute | solution.py:30
  155.4 4.2 %shard_map.75 = (bf16[2,96,896]{2,1,0:T(8,128)(2,1)S(1)}, bf16[2,96,896]{2,1,0:T(8,128)(2,1)S(1)}, bf16[2,96,896]{2,1,0:T(8,128)(2,1)S(1)}, bf16[2,96,896]{2,1,0:T(8,128)(2,1)S(1)}) custom-call(s32[4]{0:T(128)S(1)} %pad_add_fusion.at_ref, bf16[4,96,1024]{2,1,0:T(8,128)(2,1)S(1)} %pad_maximum_fusion.1.own_ref, ...), custom_call_target="tpu_custom_call" | custom-call | bytes 16384 | tf_op jit(solution)/shard_map/pallas_call | solution.py:279
  165.3 3.6 %collective-permute-done.24 = bf16[128,896]{1,0:T(8,128)(2,1)S(1)} collective-permute-done((bf16[128,896]{1,0:T(8,128)(2,1)S(1)}, bf16[128,896]{1,0:T(8,128)(2,1)S(1)}, u32[]{:S(2)}, u32[]{:S(2)}) %collective-permute-start.24) | collective-permute-done | bytes 229408 | tf_op jit(solution)/shard_map/ppermute | solution.py:21
  169.3 6.2 %collective-permute-done.21.refs_2_ = bf16[2,96,896]{2,1,0:T(8,128)(2,1)S(1)} collective-permute-done((bf16[2,96,896]{2,1,0:T(8,128)(2,1)S(1)}, bf16[2,96,896]{2,1,0:T(8,128)(2,1)S(1)}, u32[]{:S(2)}, u32[]{:S(2)}) %collective-permute-start.21) | collective-permute-done | bytes 344096 | tf_op jit(solution)/shard_map/ppermute | solution.py:21
  179.0 3.7 %collective-permute-start.25 = (bf16[128,896]{1,0:T(8,128)(2,1)S(1)}, bf16[128,896]{1,0:T(8,128)(2,1)S(1)}, u32[]{:S(2)}, u32[]{:S(2)}) collective-permute-start(bf16[128,896]{1,0:T(8,128)(2,1)S(1)} %get-tuple-element.84), channel_id=1, source_target_pairs={{0,16},{1,17},{2,18},{3,19},{4,20},{5,21},{6,22},{7,23},{8,24},{9,... | collective-permute-start | bytes 688136 | tf_op jit(solution)/shard_map/ppermute | solution.py:21
  184.5 8.7 %collective-permute-done.25 = bf16[128,896]{1,0:T(8,128)(2,1)S(1)} collective-permute-done((bf16[128,896]{1,0:T(8,128)(2,1)S(1)}, bf16[128,896]{1,0:T(8,128)(2,1)S(1)}, u32[]{:S(2)}, u32[]{:S(2)}) %collective-permute-start.25) | collective-permute-done | bytes 229408 | tf_op jit(solution)/shard_map/ppermute | solution.py:21
  193.2 3.8 %collective-permute-done.27 = bf16[128,896]{1,0:T(8,128)(2,1)S(1)} collective-permute-done((bf16[128,896]{1,0:T(8,128)(2,1)S(1)}, bf16[128,896]{1,0:T(8,128)(2,1)S(1)}, u32[]{:S(2)}, u32[]{:S(2)}) %collective-permute-start.27) | collective-permute-done | bytes 229408 | tf_op jit(solution)/shard_map/ppermute | solution.py:21
  (68 shorter events, 63.1 us)
Async XLA Ops:
  1.0 11.4 %collective-permute-start.3 = (bf16[144,896]{1,0:T(8,128)(2,1)S(1)}, bf16[144,896]{1,0:T(8,128)(2,1)S(1)}, u32[]{:S(2)}, u32[]{:S(2)}) collective-permute-start(bf16[144,896]{1,0:T(8,128)(2,1)S(1)} %shard_map.64.refs_0_), channel_id=1, source_target_pairs={{0,28},{1,29},{2,30},{3,31},{4,0},{5,1},{6,2},{7,3},{8,4},{9,5},{1... | collective-permute-start | bytes 774152 | tf_op jit(solution)/shard_map/ppermute | solution.py:21
  7.5 8.3 %collective-permute-start = (bf16[144,896]{1,0:T(8,128)(2,1)S(1)}, bf16[144,896]{1,0:T(8,128)(2,1)S(1)}, u32[]{:S(2)}, u32[]{:S(2)}) collective-permute-start(bf16[144,896]{1,0:T(8,128)(2,1)S(1)} %shard_map.64.refs_0_), channel_id=1, source_target_pairs={{0,4},{1,5},{2,6},{3,7},{4,8},{5,9},{6,10},{7,11},{8,12},{9,13},{1... | collective-permute-start | bytes 774152 | tf_op jit(solution)/shard_map/ppermute | solution.py:21
  32.3 14.4 %collective-permute-start.10 = (bf16[144,896]{1,0:T(8,128)(2,1)S(1)}, bf16[144,896]{1,0:T(8,128)(2,1)S(1)}, u32[]{:S(2)}, u32[]{:S(2)}) collective-permute-start(bf16[144,896]{1,0:T(8,128)(2,1)S(1)} %shard_map.64.refs_0_), channel_id=1, source_target_pairs={{0,16},{1,17},{2,18},{3,19},{4,20},{5,21},{6,22},{7,23},{8,24},{9,... | collective-permute-start | bytes 774152 | tf_op jit(solution)/shard_map/ppermute | solution.py:21
  34.0 18.1 %all-to-all-start = ((bf16[4,192,896]{2,1,0:T(8,128)(2,1)}), bf16[4,192,896]{2,1,0:T(8,128)(2,1)S(1)}, u32[]{:S(2)}, u32[]{:S(2)}) async-start(bf16[4,192,896]{2,1,0:T(8,128)(2,1)} %get-tuple-element.49), calls=%async_computation | async-start | bytes 2752512 | tf_op jit(solution)/shard_map/all_to_all | solution.py:217
  52.1 23.6 %all-to-all-start.1 = ((bf16[4,192,896]{2,1,0:T(8,128)(2,1)}), bf16[4,192,896]{2,1,0:T(8,128)(2,1)S(1)}, u32[]{:S(2)}, u32[]{:S(2)}) async-start(bf16[4,192,896]{2,1,0:T(8,128)(2,1)} %get-tuple-element.55), calls=%async_computation.1 | async-start | bytes 2752512 | tf_op jit(solution)/shard_map/all_to_all | solution.py:217
  59.8 9.7 %collective-permute-start.6 = (bf16[4,2,96,1024]{3,2,1,0:T(8,128)(2,1)S(1)}, bf16[4,2,96,1024]{3,2,1,0:T(8,128)(2,1)S(1)}, u32[]{:S(2)}, u32[]{:S(2)}) collective-permute-start(bf16[4,2,96,1024]{3,2,1,0:T(8,128)(2,1)S(1)} %shard_map.67), channel_id=1, source_target_pairs={{0,32},{32,0},{64,96},{96,64},{128,160},{160,128},{192,224},{224,1... | collective-permute-start | bytes 4718600 | tf_op jit(solution)/shard_map/ppermute | solution.py:30
  70.8 14.3 %collective-permute-start.7 = (bf16[2,96,1024]{2,1,0:T(8,128)(2,1)}, bf16[2,96,1024]{2,1,0:T(8,128)(2,1)S(1)}, u32[]{:S(2)}, u32[]{:S(2)}) collective-permute-start(bf16[2,96,1024]{2,1,0:T(8,128)(2,1)} %get-tuple-element.51), channel_id=1, source_target_pairs={{0,64},{32,96},{64,128},{96,160},{128,192},{160,224},{192,0},{224,... | collective-permute-start | bytes 1179656 | tf_op jit(solution)/shard_map/ppermute | solution.py:30
  72.1 20.5 %collective-permute-start.8 = (bf16[2,96,1024]{2,1,0:T(8,128)(2,1)}, bf16[2,96,1024]{2,1,0:T(8,128)(2,1)S(1)}, u32[]{:S(2)}, u32[]{:S(2)}) collective-permute-start(bf16[2,96,1024]{2,1,0:T(8,128)(2,1)} %get-tuple-element.52), channel_id=1, source_target_pairs={{0,128},{32,160},{64,192},{96,224},{128,0},{160,32},{192,64},{224,... | collective-permute-start | bytes 1179656 | tf_op jit(solution)/shard_map/ppermute | solution.py:30
  74.7 17.9 %collective-permute-start.9 = (bf16[2,96,1024]{2,1,0:T(8,128)(2,1)S(1)}, bf16[2,96,1024]{2,1,0:T(8,128)(2,1)S(1)}, u32[]{:S(2)}, u32[]{:S(2)}) collective-permute-start(bf16[2,96,1024]{2,1,0:T(8,128)(2,1)S(1)} %get-tuple-element.53), channel_id=1, source_target_pairs={{0,192},{32,224},{64,0},{96,32},{128,64},{160,96},{192,128},{224,1... | collective-permute-start | bytes 1179656 | tf_op jit(solution)/shard_map/ppermute | solution.py:30
  79.9 12.7 %collective-permute-start.11 = (bf16[4,2,96,1024]{3,2,1,0:T(8,128)(2,1)S(1)}, bf16[4,2,96,1024]{3,2,1,0:T(8,128)(2,1)S(1)}, u32[]{:S(2)}, u32[]{:S(2)}) collective-permute-start(bf16[4,2,96,1024]{3,2,1,0:T(8,128)(2,1)S(1)} %shard_map.71), channel_id=1, source_target_pairs={{0,32},{32,0},{64,96},{96,64},{128,160},{160,128},{192,224},{224,1... | collective-permute-start | bytes 4718600 | tf_op jit(solution)/shard_map/ppermute | solution.py:30
  93.2 15.3 %collective-permute-start.12 = (bf16[3,96,1024]{2,1,0:T(8,128)(2,1)S(1)}, bf16[3,96,1024]{2,1,0:T(8,128)(2,1)S(1)}, u32[]{:S(2)}, u32[]{:S(2)}) collective-permute-start(bf16[3,96,1024]{2,1,0:T(8,128)(2,1)S(1)} %get-tuple-element.58), channel_id=1, source_target_pairs={{0,64},{32,96},{64,128},{96,160},{128,192},{160,224},{192,0},{224,... | collective-permute-start | bytes 1769480 | tf_op jit(solution)/shard_map/ppermute | solution.py:30
  93.4 28.8 %collective-permute-start.13 = (bf16[3,96,1024]{2,1,0:T(8,128)(2,1)S(1)}, bf16[3,96,1024]{2,1,0:T(8,128)(2,1)S(1)}, u32[]{:S(2)}, u32[]{:S(2)}) collective-permute-start(bf16[3,96,1024]{2,1,0:T(8,128)(2,1)S(1)} %get-tuple-element.59), channel_id=1, source_target_pairs={{0,128},{32,160},{64,192},{96,224},{128,0},{160,32},{192,64},{224,... | collective-permute-start | bytes 1769480 | tf_op jit(solution)/shard_map/ppermute | solution.py:30
  96.6 25.6 %collective-permute-start.14 = (bf16[3,96,1024]{2,1,0:T(8,128)(2,1)S(1)}, bf16[3,96,1024]{2,1,0:T(8,128)(2,1)S(1)}, u32[]{:S(2)}, u32[]{:S(2)}) collective-permute-start(bf16[3,96,1024]{2,1,0:T(8,128)(2,1)S(1)} %get-tuple-element.60), channel_id=1, source_target_pairs={{0,192},{32,224},{64,0},{96,32},{128,64},{160,96},{192,128},{224,1... | collective-permute-start | bytes 1769480 | tf_op jit(solution)/shard_map/ppermute | solution.py:30
  131.0 22.5 %all-to-all-start.2 = ((bf16[4,2,96,896]{3,2,1,0:T(8,128)(2,1)}), bf16[4,2,96,896]{3,2,1,0:T(8,128)(2,1)S(1)}, u32[]{:S(2)}, u32[]{:S(2)}) async-start(bf16[4,2,96,896]{3,2,1,0:T(8,128)(2,1)} %shard_map.74), calls=%async_computation.2 | async-start | bytes 2752512 | tf_op jit(solution)/shard_map/all_to_all | solution.py:217
  138.6 11.8 %collective-permute-start.15 = (bf16[96,1024]{1,0:T(8,128)(2,1)S(1)}, bf16[96,1024]{1,0:T(8,128)(2,1)S(1)}, u32[]{:S(2)}, u32[]{:S(2)}) collective-permute-start(bf16[96,1024]{1,0:T(8,128)(2,1)S(1)} %shard_map.73), channel_id=1, source_target_pairs={{0,64},{32,96},{64,128},{96,160},{128,192},{160,224},{192,0},{224,... | collective-permute-start | bytes 589832 | tf_op jit(solution)/shard_map/ppermute | solution.py:30
  155.1 8.9 %collective-permute-start.23 = (bf16[128,896]{1,0:T(8,128)(2,1)S(1)}, bf16[128,896]{1,0:T(8,128)(2,1)S(1)}, u32[]{:S(2)}, u32[]{:S(2)}) collective-permute-start(bf16[128,896]{1,0:T(8,128)(2,1)S(1)} %get-tuple-element.74), channel_id=1, source_target_pairs={{0,28},{1,29},{2,30},{3,31},{4,0},{5,1},{6,2},{7,3},{8,4},{9,5},{1... | collective-permute-start | bytes 688136 | tf_op jit(solution)/shard_map/ppermute | solution.py:21
  159.7 9.6 %collective-permute-start.20 = (bf16[2,96,896]{2,1,0:T(8,128)(2,1)S(1)}, bf16[2,96,896]{2,1,0:T(8,128)(2,1)S(1)}, u32[]{:S(2)}, u32[]{:S(2)}) collective-permute-start(bf16[2,96,896]{2,1,0:T(8,128)(2,1)S(1)} %get-tuple-element.68), channel_id=1, source_target_pairs={{0,1},{1,2},{2,3},{3,0},{4,5},{5,6},{6,7},{7,4},{8,9},{9,10},{10,1... | collective-permute-start | bytes 1032200 | tf_op jit(solution)/shard_map/ppermute | solution.py:21
  160.0 15.5 %collective-permute-start.21 = (bf16[2,96,896]{2,1,0:T(8,128)(2,1)S(1)}, bf16[2,96,896]{2,1,0:T(8,128)(2,1)S(1)}, u32[]{:S(2)}, u32[]{:S(2)}) collective-permute-start(bf16[2,96,896]{2,1,0:T(8,128)(2,1)S(1)} %get-tuple-element.69), channel_id=1, source_target_pairs={{0,2},{1,3},{2,0},{3,1},{4,6},{5,7},{6,4},{7,5},{8,10},{9,11},{10,... | collective-permute-start | bytes 1032200 | tf_op jit(solution)/shard_map/ppermute | solution.py:21
  161.8 15.7 %collective-permute-start.22 = (bf16[2,96,896]{2,1,0:T(8,128)(2,1)S(1)}, bf16[2,96,896]{2,1,0:T(8,128)(2,1)S(1)}, u32[]{:S(2)}, u32[]{:S(2)}) collective-permute-start(bf16[2,96,896]{2,1,0:T(8,128)(2,1)S(1)} %get-tuple-element.70), channel_id=1, source_target_pairs={{0,3},{1,0},{2,1},{3,2},{4,7},{5,4},{6,5},{7,6},{8,11},{9,8},{10,9... | collective-permute-start | bytes 1032200 | tf_op jit(solution)/shard_map/ppermute | solution.py:21
  164.0 18.7 %collective-permute-start.26 = (bf16[128,896]{1,0:T(8,128)(2,1)S(1)}, bf16[128,896]{1,0:T(8,128)(2,1)S(1)}, u32[]{:S(2)}, u32[]{:S(2)}) collective-permute-start(bf16[128,896]{1,0:T(8,128)(2,1)S(1)} %add_convert_fusion.4), channel_id=1, source_target_pairs={{0,28},{1,29},{2,30},{3,31},{4,0},{5,1},{6,2},{7,3},{8,4},{9,5},{1... | collective-permute-start | bytes 688136 | tf_op jit(solution)/shard_map/ppermute | solution.py:21
  169.0 13.9 %collective-permute-start.28 = (bf16[128,896]{1,0:T(8,128)(2,1)S(1)}, bf16[128,896]{1,0:T(8,128)(2,1)S(1)}, u32[]{:S(2)}, u32[]{:S(2)}) collective-permute-start(bf16[128,896]{1,0:T(8,128)(2,1)S(1)} %add_convert_fusion.3), channel_id=1, source_target_pairs={{0,4},{1,5},{2,6},{3,7},{4,8},{5,9},{6,10},{7,11},{8,12},{9,13},{1... | collective-permute-start | bytes 688136 | tf_op jit(solution)/shard_map/ppermute | solution.py:21
  179.0 14.2 %collective-permute-start.25 = (bf16[128,896]{1,0:T(8,128)(2,1)S(1)}, bf16[128,896]{1,0:T(8,128)(2,1)S(1)}, u32[]{:S(2)}, u32[]{:S(2)}) collective-permute-start(bf16[128,896]{1,0:T(8,128)(2,1)S(1)} %get-tuple-element.84), channel_id=1, source_target_pairs={{0,16},{1,17},{2,18},{3,19},{4,20},{5,21},{6,22},{7,23},{8,24},{9,... | collective-permute-start | bytes 688136 | tf_op jit(solution)/shard_map/ppermute | solution.py:21
  182.8 14.2 %collective-permute-start.27 = (bf16[128,896]{1,0:T(8,128)(2,1)S(1)}, bf16[128,896]{1,0:T(8,128)(2,1)S(1)}, u32[]{:S(2)}, u32[]{:S(2)}) collective-permute-start(bf16[128,896]{1,0:T(8,128)(2,1)S(1)} %add_convert_fusion.2), channel_id=1, source_target_pairs={{0,28},{1,29},{2,30},{3,31},{4,0},{5,1},{6,2},{7,3},{8,4},{9,5},{1... | collective-permute-start | bytes 688136 | tf_op jit(solution)/shard_map/ppermute | solution.py:21
  183.0 14.7 %collective-permute-start.29 = (bf16[128,896]{1,0:T(8,128)(2,1)S(1)}, bf16[128,896]{1,0:T(8,128)(2,1)S(1)}, u32[]{:S(2)}, u32[]{:S(2)}) collective-permute-start(bf16[128,896]{1,0:T(8,128)(2,1)S(1)} %add_convert_fusion.1), channel_id=1, source_target_pairs={{0,4},{1,5},{2,6},{3,7},{4,8},{5,9},{6,10},{7,11},{8,12},{9,13},{1... | collective-permute-start | bytes 688136 | tf_op jit(solution)/shard_map/ppermute | solution.py:21
  (9 other events, 56.1 us)
